TPU v7x, 512 devices: a whole 4x4x16 slice. The times are simulated.
512 devices in a mesh: ctx: 64 (over z, x), tp: 8 (over y, core).
Axes of the slice: x: 4, y: 4, z: 16, core: 2. Of those that a mesh axis runs over, the one named last changes fastest.
Arguments:
- features: bfloat16 [8192, 3, 4096], P('ctx', None, 'tp'), may hold values from -6 to 6
- short_filter: float32 [3, 3, 4096], P(None, None, 'tp'), may hold values from -3 to 3
- long_filter: float32 [8192, 4096], P('ctx', 'tp'), may hold values from -1.0558378 to 1.0558378
- filter_bias: float32 [4096], P('tp'), may hold values from -4 to 4
- out_weight: bfloat16 [4096, 4096], P('tp'), may hold values from -0.09375 to 0.09375
Outputs:
- mixed: bfloat16 [8192, 4096], P('ctx', 'tp')
All inputs are finite; a program needn't handle non-finite values.
Results may differ from a plain program's by a relative error of at most 0.0049.
Values may be sent and summed in bfloat16 or wider, within the bound.
No kernel may reach another device: no remote copies, remote signals or barrier semaphores. Data moves between devices by JAX's collectives and lax.ppermute only.
A program may use at most 64 MiB of HBM per device.

v0:
```python
import math

import jax
import jax.numpy as jnp
import numpy as np
from jax import lax
from jax.sharding import PartitionSpec as P

highest = lax.Precision.HIGHEST


def shifted(block, axis, distance):
    devices = range(lax.axis_size(axis))
    route = [(i - distance, i) for i in devices if i - distance in devices]
    return lax.ppermute(block, axis, route)


def angle_table(left_idx, right_idx, modulus, sign_scale):
    turns = left_idx[:, None] * right_idx[None, :] % modulus
    angles = 2.0 * math.pi * turns / modulus
    return (
        jnp.asarray(np.cos(angles) * sign_scale, jnp.float32),
        jnp.asarray(np.sin(angles) * sign_scale, jnp.float32),
    )


def body(features, short_filter, long_filter, filter_bias, out_weight):
    tok_rows = features.shape[0]
    ch_local = features.shape[2]
    ctx_count = lax.axis_size("ctx")
    my_index = lax.axis_index("ctx")
    total_len = 2 * ctx_count * tok_rows
    rim_rows = shifted(features[tok_rows - 2 :], "ctx", 1)
    extended = jnp.concatenate([rim_rows, features], axis=0).astype(jnp.float32)
    current = features.astype(jnp.float32)
    featurized = (
        short_filter[0] * current
        + short_filter[1] * extended[1 : tok_rows + 1]
        + short_filter[2] * extended[:tok_rows]
    )
    query_part = featurized[:, 0]
    key_part = featurized[:, 1]
    value_part = featurized[:, 2]
    gate_in = key_part * value_part
    signals = jnp.concatenate([gate_in, long_filter], axis=1)
    columns = lax.all_to_all(
        signals.reshape(1, tok_rows, 2 * ch_local), "ctx", split_axis=1, concat_axis=0, tiled=True
    )
    kc_order = np.arange(ctx_count)
    slot_freq = 2 * np.repeat(kc_order, 2) + np.tile(np.arange(2), ctx_count)
    cos_first, sin_first = angle_table(slot_freq, np.arange(ctx_count), 2 * ctx_count, 1.0)
    spec_re = jnp.einsum("mc,crk->mrk", cos_first, columns, precision=highest)
    spec_im = -jnp.einsum("mc,crk->mrk", sin_first, columns, precision=highest)
    spec_re, spec_im = (
        lax.all_to_all(spec_re, "ctx", split_axis=0, concat_axis=1, tiled=True),
        lax.all_to_all(spec_im, "ctx", split_axis=0, concat_axis=1, tiled=True),
    )
    pos_local = jnp.arange(tok_rows, dtype=jnp.int32)
    freq_pair = 2 * my_index + jnp.arange(2, dtype=jnp.int32)
    turn_count = freq_pair[:, None] * pos_local[None, :] % total_len
    phase_angle = 2.0 * math.pi / total_len * turn_count.astype(jnp.float32)
    tw_cos = jnp.cos(phase_angle)[:, :, None]
    tw_sin = jnp.sin(phase_angle)[:, :, None]
    twisted_re = spec_re * tw_cos + spec_im * tw_sin
    twisted_im = spec_im * tw_cos - spec_re * tw_sin
    inner_idx = np.arange(tok_rows)
    cos_local, sin_local = angle_table(inner_idx, inner_idx, tok_rows, 1.0)
    freq_re = jnp.einsum("kr,erc->ekc", cos_local, twisted_re, precision=highest) + jnp.einsum(
        "kr,erc->ekc", sin_local, twisted_im, precision=highest
    )
    freq_im = jnp.einsum("kr,erc->ekc", cos_local, twisted_im, precision=highest) - jnp.einsum(
        "kr,erc->ekc", sin_local, twisted_re, precision=highest
    )
    gate_re = freq_re[..., :ch_local]
    gate_im = freq_im[..., :ch_local]
    filt_re = freq_re[..., ch_local:]
    filt_im = freq_im[..., ch_local:]
    prod_re = gate_re * filt_re - gate_im * filt_im
    prod_im = gate_re * filt_im + gate_im * filt_re
    back_re = jnp.einsum("rk,ekc->erc", cos_local, prod_re, precision=highest) - jnp.einsum(
        "rk,ekc->erc", sin_local, prod_im, precision=highest
    )
    back_im = jnp.einsum("rk,ekc->erc", cos_local, prod_im, precision=highest) + jnp.einsum(
        "rk,ekc->erc", sin_local, prod_re, precision=highest
    )
    turned_re = back_re * tw_cos - back_im * tw_sin
    turned_im = back_re * tw_sin + back_im * tw_cos
    gathered_re, gathered_im = (
        lax.all_to_all(turned_re, "ctx", split_axis=1, concat_axis=0, tiled=True),
        lax.all_to_all(turned_im, "ctx", split_axis=1, concat_axis=0, tiled=True),
    )
    cos_last, sin_last = angle_table(
        np.arange(ctx_count), np.arange(2 * ctx_count), 2 * ctx_count, 1.0 / total_len
    )
    by_block = jnp.einsum("cm,mrk->crk", cos_last, gathered_re, precision=highest) - jnp.einsum(
        "cm,mrk->crk", sin_last, gathered_im, precision=highest
    )
    long_conv = lax.all_to_all(by_block, "ctx", split_axis=0, concat_axis=1, tiled=True).reshape(
        tok_rows, ch_local
    )
    conv_out = long_conv + filter_bias * gate_in
    gated = (query_part * conv_out).astype(jnp.bfloat16)
    partial_cols = lax.psum_scatter(
        lax.dot_general(
            out_weight, gated, (((0,), (1,)), ((), ())), preferred_element_type=jnp.float32
        ),
        "tp",
        scatter_dimension=0,
        tiled=True,
    )
    return partial_cols.T.astype(jnp.bfloat16)


def solution(mesh):
    in_specs = (P("ctx", None, "tp"), P(None, None, "tp"), P("ctx", "tp"), P("tp"), P("tp", None))
    out_specs = P("ctx", "tp")
    return jax.shard_map(body, mesh=mesh, in_specs=in_specs, out_specs=out_specs, check_vma=False)
```

profile of v0, /device:TPU:1, one launch (start us, length us, event | category | flops | bytes accessed | tf_op | source)
XLA Modules:
  0.0 350.7 jit_solution(17359928191571336732)
XLA Ops:
  6.5 0.8 slice.41
  7.3 3.9 %collective-permute-start = (bf16[2,3,512]{2,0,1:T(2,128)(2,1)S(1)}, bf16[2,3,512]{2,0,1:T(2,128)(2,1)S(1)}, u32[]{:S(2)}, u32[]{:S(2)}) collective-permute-start(bf16[2,3,512]{2,0,1:T(2,128)(2,1)S(1)} %slice.41), channel_id=1, source_target_pairs={{0,8},{8,16},{16,24},{24,32},{32,40},{40,48},{48,56},{56,64},{64,7... | collective-permute-start | bytes 18440 | tf_op jit(solution)/shard_map/ppermute | solution.py:15
  12.0 1.1 maximum_convert_fusion
  13.2 1.2 fusion.6
  14.4 0.9 copy-done
  15.9 48.4 %all_to_all.93 = f32[1,128,1024]{2,0,1:T(1,128)S(1)} all-to-all(f32[1,128,1024]{2,0,1:T(1,128)S(1)} %copy.30), channel_id=1, replica_groups=mesh['ctx'=64,'tp'=8] {'ctx'}, dimensions={1} | all-to-all | bytes 1048576 | tf_op jit(solution)/shard_map/all_to_all | solution.py:46
  64.3 1.2 reduce
  65.9 1.8 fusion
  67.7 1.3 copy.36
  69.0 8.9 %all-to-all-start.2 = ((f32[128,2,1024]{2,1,0:T(2,128)}), f32[128,2,1024]{2,1,0:T(2,128)S(1)}, u32[]{:S(2)}, u32[]{:S(2)}) async-start(f32[128,2,1024]{2,1,0:T(2,128)} %copy.36), calls=%async_computation.2 | async-start | bytes 2097152 | tf_op jit(solution)/shard_map/all_to_all | solution.py:56
  78.0 1.1 fusion.12
  79.1 1.8 copy.32
  80.9 47.9 %all-to-all-done.2 = f32[128,2,1024]{2,1,0:T(2,128)S(1)} async-done(((f32[128,2,1024]{2,1,0:T(2,128)}), f32[128,2,1024]{2,1,0:T(2,128)S(1)}, u32[]{:S(2)}, u32[]{:S(2)}) %all-to-all-start.2) | async-done | bytes 1048608 | tf_op jit(solution)/shard_map/all_to_all | solution.py:56
  128.8 8.8 %all-to-all-start.1 = ((f32[128,2,1024]{2,1,0:T(2,128)}), f32[128,2,1024]{2,1,0:T(2,128)S(1)}, u32[]{:S(2)}, u32[]{:S(2)}) async-start(f32[128,2,1024]{2,1,0:T(2,128)} %copy.32), calls=%async_computation.1 | async-start | bytes 2097152 | tf_op jit(solution)/shard_map/all_to_all | solution.py:55
  137.9 0.7 copy.38
  139.2 47.7 %all-to-all-done.1 = f32[128,2,1024]{2,1,0:T(2,128)S(1)} async-done(((f32[128,2,1024]{2,1,0:T(2,128)}), f32[128,2,1024]{2,1,0:T(2,128)S(1)}, u32[]{:S(2)}, u32[]{:S(2)}) %all-to-all-start.1) | async-done | bytes 1048608 | tf_op jit(solution)/shard_map/all_to_all | solution.py:55
  187.4 2.7 fusion.4
  190.7 1.5 copy.40
  192.2 1.0 fusion.25
  193.2 1.0 fusion.24
  194.2 1.0 fusion.1
  195.2 1.0 fusion.2
  198.7 1.0 copy.46
  199.7 9.6 %all-to-all-start.4 = ((f32[2,128,512]{2,0,1:T(2,128)}), f32[2,128,512]{2,0,1:T(2,128)S(1)}, u32[]{:S(2)}, u32[]{:S(2)}) async-start(f32[2,128,512]{2,0,1:T(2,128)} %copy.46), calls=%async_computation.4 | async-start | bytes 1048576 | tf_op jit(solution)/shard_map/all_to_all | solution.py:90
  209.3 1.0 copy.43
  210.3 27.1 %all-to-all-done.4 = f32[2,128,512]{2,0,1:T(2,128)S(1)} async-done(((f32[2,128,512]{2,0,1:T(2,128)}), f32[2,128,512]{2,0,1:T(2,128)S(1)}, u32[]{:S(2)}, u32[]{:S(2)}) %all-to-all-start.4) | async-done | bytes 524320 | tf_op jit(solution)/shard_map/all_to_all | solution.py:90
  237.4 8.7 %all-to-all-start.3 = ((f32[2,128,512]{2,0,1:T(2,128)}), f32[2,128,512]{2,0,1:T(2,128)S(1)}, u32[]{:S(2)}, u32[]{:S(2)}) async-start(f32[2,128,512]{2,0,1:T(2,128)} %copy.43), calls=%async_computation.3 | async-start | bytes 1048576 | tf_op jit(solution)/shard_map/all_to_all | solution.py:89
  246.8 27.5 %all-to-all-done.3 = f32[2,128,512]{2,0,1:T(2,128)S(1)} async-done(((f32[2,128,512]{2,0,1:T(2,128)}), f32[2,128,512]{2,0,1:T(2,128)S(1)}, u32[]{:S(2)}, u32[]{:S(2)}) %all-to-all-start.3) | async-done | bytes 524320 | tf_op jit(solution)/shard_map/all_to_all | solution.py:89
  275.9 26.2 %all_to_all.94 = f32[64,2,512]{2,1,0:T(2,128)S(1)} all-to-all(f32[64,2,512]{2,1,0:T(2,128)S(1)} %copy.49), channel_id=1, replica_groups=mesh['ctx'=64,'tp'=8] {'ctx'}, dimensions={0} | all-to-all | bytes 524288 | tf_op jit(solution)/shard_map/all_to_all | solution.py:98
  302.3 4.4 %convolution_bitcast_fusion = f32[4096,128]{0,1:T(8,128)} fusion(bf16[512,4096]{1,0:T(8,128)(2,1)} %param.15, f32[128,3,512]{2,0,1:T(8,128)} %copy-done, f32[128,512]{1,0:T(8,128)S(1)} %reshape.73, f32[128,512]{1,0:T(8,128)S(1)} %fusion.14, f32[512]{0:T(512)S(1)} %copy-done.8), kind=kOutput, calls=%fused_computation | convolution fusion | flops 537133056 | bytes 7079936 | tf_op jit(solution)/shard_map/dot_general | solution.py:104
  306.7 35.5 %reduce-scatter.2.cloned.1.call-done = f32[512,128]{0,1:T(8,128)} async-done(((f32[4096,128]{0,1:T(8,128)}), f32[512,128]{0,1:T(8,128)}) %reduce-scatter.2.cloned.1.call-update) | async-done | bytes 262160 | tf_op jit(solution)/shard_map/reduce_scatter | solution.py:103
  342.3 1.6 convert_bitcast_fusion
  (44 shorter events, 8.5 us)
Async XLA Ops:
  6.5 8.8 %copy-start.3 = (f32[128,512]{1,0:T(8,128)S(1)}, f32[128,512]{1,0:T(8,128)}, u32[]{:S(2)}) copy-start(f32[128,512]{1,0:T(8,128)} %param.13) | copy-start | bytes 786436
  7.3 4.7 %collective-permute-start = (bf16[2,3,512]{2,0,1:T(2,128)(2,1)S(1)}, bf16[2,3,512]{2,0,1:T(2,128)(2,1)S(1)}, u32[]{:S(2)}, u32[]{:S(2)}) collective-permute-start(bf16[2,3,512]{2,0,1:T(2,128)(2,1)S(1)} %slice.41), channel_id=1, source_target_pairs={{0,8},{8,16},{16,24},{24,32},{32,40},{40,48},{48,56},{56,64},{64,7... | collective-permute-start | bytes 18440 | tf_op jit(solution)/shard_map/ppermute | solution.py:15
  13.2 52.7 %copy-start.7 = (f32[128,64,1]{0,1,2:T(8,128)S(1)}, f32[128,64,1]{0,1,2:T(8,128)}, u32[]{:S(2)}) copy-start(f32[128,64,1]{0,1,2:T(8,128)} %constant.50) | copy-start | bytes 98308
  14.4 0.9 copy-start
  64.3 13.7 %copy-start.6 = (f32[128,64,1]{0,1,2:T(8,128)S(1)}, f32[128,64,1]{0,1,2:T(8,128)}, u32[]{:S(2)}) copy-start(f32[128,64,1]{0,1,2:T(8,128)} %constant.49) | copy-start | bytes 98308
  69.0 59.8 %all-to-all-start.2 = ((f32[128,2,1024]{2,1,0:T(2,128)}), f32[128,2,1024]{2,1,0:T(2,128)S(1)}, u32[]{:S(2)}, u32[]{:S(2)}) async-start(f32[128,2,1024]{2,1,0:T(2,128)} %copy.36), calls=%async_computation.2 | async-start | bytes 2097152 | tf_op jit(solution)/shard_map/all_to_all | solution.py:56
  128.8 58.1 %all-to-all-start.1 = ((f32[128,2,1024]{2,1,0:T(2,128)}), f32[128,2,1024]{2,1,0:T(2,128)S(1)}, u32[]{:S(2)}, u32[]{:S(2)}) async-start(f32[128,2,1024]{2,1,0:T(2,128)} %copy.32), calls=%async_computation.1 | async-start | bytes 2097152 | tf_op jit(solution)/shard_map/all_to_all | solution.py:55
  187.4 4.7 %copy-start.2 = (f32[128,128,1]{1,0,2:T(8,128)S(1)}, f32[128,128,1]{1,0,2:T(8,128)}, u32[]{:S(2)}) copy-start(f32[128,128,1]{1,0,2:T(8,128)} %constant.51) | copy-start | bytes 196612
  190.2 4.0 %copy-start.1 = (f32[128,128,1]{1,0,2:T(8,128)S(1)}, f32[128,128,1]{1,0,2:T(8,128)}, u32[]{:S(2)}) copy-start(f32[128,128,1]{1,0,2:T(8,128)} %constant.52) | copy-start | bytes 196612
  198.7 76.0 %copy-start.5 = (f32[64,128,1]{1,0,2:T(8,128)S(1)}, f32[64,128,1]{1,0,2:T(8,128)}, u32[]{:S(2)}) copy-start(f32[64,128,1]{1,0,2:T(8,128)} %constant.53) | copy-start | bytes 98308
  199.7 75.5 %copy-start.4 = (f32[64,128,1]{1,0,2:T(8,128)S(1)}, f32[64,128,1]{1,0,2:T(8,128)}, u32[]{:S(2)}) copy-start(f32[64,128,1]{1,0,2:T(8,128)} %constant.54) | copy-start | bytes 98308
  199.7 37.7 %all-to-all-start.4 = ((f32[2,128,512]{2,0,1:T(2,128)}), f32[2,128,512]{2,0,1:T(2,128)S(1)}, u32[]{:S(2)}, u32[]{:S(2)}) async-start(f32[2,128,512]{2,0,1:T(2,128)} %copy.46), calls=%async_computation.4 | async-start | bytes 1048576 | tf_op jit(solution)/shard_map/all_to_all | solution.py:90
  210.3 92.0 %copy-start.8 = (f32[512]{0:T(512)S(1)}, f32[512]{0:T(512)}, u32[]{:S(2)}) copy-start(f32[512]{0:T(512)} %param.14) | copy-start | bytes 6148
  237.4 36.9 %all-to-all-start.3 = ((f32[2,128,512]{2,0,1:T(2,128)}), f32[2,128,512]{2,0,1:T(2,128)S(1)}, u32[]{:S(2)}, u32[]{:S(2)}) async-start(f32[2,128,512]{2,0,1:T(2,128)} %copy.43), calls=%async_computation.3 | async-start | bytes 1048576 | tf_op jit(solution)/shard_map/all_to_all | solution.py:89
  246.1 96.2 %reduce-scatter.2.cloned.1.call-start = ((), (), s32[]{:S(2)}) async-start(), calls=%async_computation.7 | async-start | bytes 2359296 | tf_op jit(solution)/shard_map/reduce_scatter | solution.py:103
Sparse Core Ops, SparseCore 0:
  306.8 35.3 reduce-scatter.1
where the time goes:
time: 353 us; the launch traced here: 351 us
  waiting for transfers between devices  186 us (53%)
  blocking collectives  74.6 us (21%)
  starting transfers between devices  40.3 us (11%)
  matrix products  14.5 us (4%)
  between operations  13.8 us (4%)
  local copies, waits for them, and re-layouts  13.5 us (4%)
  other arithmetic  8.22 us (2%)
    all_to_all x1, blocking collectives, body(): lax.all_to_all(signals.reshape(1, tok_rows, 2 * ch_local), 'ctx', split_a...  48.4 us
    all_to_all x1, waiting for transfers between devices, body(): lax.all_to_all(spec_im, 'ctx', split_axis=0, concat_axis=1, tiled=True)  47.9 us
    all_to_all x1, waiting for transfers between devices, body(): lax.all_to_all(spec_re, 'ctx', split_axis=0, concat_axis=1, tiled=True)  47.7 us
    reduce_scatter x1, waiting for transfers between devices, body(): lax.psum_scatter(lax.dot_general(out_weight, gated, (((0,), (1,)), ((), (...  35.5 us
    all_to_all x1, waiting for transfers between devices, body(): lax.all_to_all(turned_re, 'ctx', split_axis=1, concat_axis=0, tiled=True)  27.5 us
    all_to_all x1, waiting for transfers between devices, body(): lax.all_to_all(turned_im, 'ctx', split_axis=1, concat_axis=0, tiled=True)  27.1 us
    all_to_all x1, blocking collectives, body(): lax.all_to_all(by_block, 'ctx', split_axis=0, concat_axis=1, tiled=True)  26.2 us
    all_to_all x1, starting transfers between devices, body(): lax.all_to_all(turned_im, 'ctx', split_axis=1, concat_axis=0, tiled=True)  9.61 us
  transfers between devices with their start and end apart: 6, of which 5 were waited for; matrix products, arithmetic and copies ran while one was open for 2% of the time, Pallas kernels for 0%

commit v1 on v0

v1 whole, which is shorter than its diff:
```python
import functools
import math

import jax
import jax.numpy as jnp
import numpy as np
from jax import lax
from jax.experimental import pallas as pl
from jax.experimental.pallas import tpu as pltpu
from jax.sharding import PartitionSpec as P

F32 = jnp.float32
BF16 = jnp.bfloat16
VMEM = pl.BlockSpec(memory_space=pltpu.VMEM)
PARAMS = pltpu.CompilerParams(vmem_limit_bytes=48 * 1024 * 1024)


def halves(table):
    high = table.astype(BF16)
    low = (table - high.astype(np.float32)).astype(BF16)
    return high, low


def tables(blocks, rows):
    length = blocks * rows
    freq = np.arange(blocks) + 0.25
    outer = 2.0 * math.pi * freq[:, None] * np.arange(blocks)[None, :] / blocks
    first = np.concatenate([np.cos(outer), -np.sin(outer)], axis=0).astype(np.float32)
    last = (np.concatenate([np.cos(outer.T), -np.sin(outer.T)], axis=1) / length).astype(np.float32)
    turn = 2.0 * math.pi * freq[:, None] * np.arange(rows)[None, :] / length
    twist = np.stack([np.cos(turn), np.sin(turn)]).astype(np.float32)
    inner = 2.0 * math.pi * (np.outer(np.arange(rows), np.arange(rows)) % rows) / rows
    cos, sin = np.cos(inner), np.sin(inner)
    forward = np.block([[cos, -sin], [sin, cos]]).astype(np.float32)
    backward = np.block([[cos, sin], [-sin, cos]]).astype(np.float32)
    first_hi, first_lo = halves(first)
    last_hi, last_lo = halves(last)
    forward_hi, forward_lo = halves(forward)
    backward_hi, backward_lo = halves(backward)
    return (
        np.concatenate([first_hi, first_lo], axis=1),
        twist,
        np.concatenate([forward_hi, forward_hi, forward_lo], axis=0),
        np.concatenate([backward_hi, backward_hi, backward_lo], axis=0),
        np.concatenate([last_hi, last_hi, last_lo], axis=1),
    )


def split(value):
    high = value.astype(BF16)
    return high, (value - high.astype(F32)).astype(BF16)


def short_kernel(features, rim, taps, filt, bias, send, query, skip):
    row = lax.broadcasted_iota(jnp.int32, features.shape[1:], 0)

    def stream(j):
        current = features[j].astype(F32)
        before = rim[j].astype(F32)
        one = jnp.where(row == 0, before[1:2], pltpu.roll(current, 1, 0))
        two = jnp.where(row == 0, before[0:1], jnp.where(row == 1, before[1:2], pltpu.roll(current, 2, 0)))
        return taps[0, j : j + 1] * current + taps[1, j : j + 1] * one + taps[2, j : j + 1] * two

    gate = stream(1) * stream(2)
    groups, both, rows = send.shape
    each = both // 2
    parts = [gate.T.reshape(groups, each, rows), filt[...].T.reshape(groups, each, rows)]
    send[...] = jnp.concatenate(parts, axis=1).astype(send.dtype)
    query[...] = stream(0).T
    skip[...] = (bias[...] * gate).T


def conv_kernel(columns, first, twist, forward, backward, last, out, gathered, spread):
    blocks, both, rows = columns.shape
    each = both // 2
    gathered[...] = columns[...].astype(F32).reshape(blocks * both, rows)
    wide = jnp.concatenate(
        [gathered[pl.ds(ch, blocks, stride=both), :] for ch in range(both)], axis=1
    ).astype(BF16)
    outer = jnp.dot(first[...], jnp.concatenate([wide, wide], axis=0), preferred_element_type=F32)
    cos, sin = twist[0], twist[1]
    twisted = []
    for ch in range(both):
        re = outer[:blocks, ch * rows : (ch + 1) * rows]
        im = outer[blocks:, ch * rows : (ch + 1) * rows]
        twisted.append(jnp.concatenate([re * cos + im * sin, im * cos - re * sin], axis=1))
    high, low = split(jnp.concatenate(twisted, axis=0))
    spectrum = jnp.dot(jnp.concatenate([high, low, high], axis=1), forward[...], preferred_element_type=F32)
    gate, filt = spectrum[: each * blocks], spectrum[each * blocks :]
    gate_re, gate_im = gate[:, :rows], gate[:, rows:]
    filt_re, filt_im = filt[:, :rows], filt[:, rows:]
    product = jnp.concatenate(
        [gate_re * filt_re - gate_im * filt_im, gate_re * filt_im + gate_im * filt_re], axis=1
    )
    high, low = split(product)
    inner = jnp.dot(jnp.concatenate([high, low, high], axis=1), backward[...], preferred_element_type=F32)
    turned = []
    for ch in range(each):
        re = inner[ch * blocks : (ch + 1) * blocks, :rows]
        im = inner[ch * blocks : (ch + 1) * blocks, rows:]
        turned.append(jnp.concatenate([re * cos - im * sin, re * sin + im * cos], axis=0))
    high, low = split(jnp.concatenate(turned, axis=1))
    result = jnp.dot(last[...], jnp.concatenate([high, low, high], axis=0), preferred_element_type=F32)
    for ch in range(each):
        spread[pl.ds(ch, blocks, stride=each), :] = result[:, ch * rows : (ch + 1) * rows]
    out[...] = spread[...].reshape(out.shape).astype(out.dtype)


def mix_kernel(conv, query, skip, weight, out, gated):
    @pl.when(pl.program_id(0) == 0)
    def _():
        conv_out = conv[...].astype(F32).reshape(query.shape) + skip[...]
        gated[...] = (query[...] * conv_out).T.astype(BF16)

    out[0] = jnp.dot(gated[...], weight[...], preferred_element_type=F32).astype(out.dtype)


def sum_kernel(parts, out):
    out[...] = jnp.sum(parts[...].astype(F32), axis=0).astype(out.dtype)


def body(features, short_filter, long_filter, filter_bias, out_weight):
    rows, streams, width = features.shape
    blocks = lax.axis_size("ctx")
    shares = lax.axis_size("tp")
    each = width // blocks
    cols = out_weight.shape[1] // shares
    planes = jnp.transpose(features, (1, 0, 2))
    route = [(i, i + 1) for i in range(blocks - 1)]
    rim = lax.ppermute(planes[:, rows - 2 :], "ctx", route)
    send, query, skip = pl.pallas_call(
        short_kernel,
        out_shape=(
            jax.ShapeDtypeStruct((blocks, 2 * each, rows), BF16),
            jax.ShapeDtypeStruct((width, rows), F32),
            jax.ShapeDtypeStruct((width, rows), F32),
        ),
        in_specs=[VMEM] * 5,
        out_specs=(VMEM, VMEM, VMEM),
        compiler_params=PARAMS,
        name="short",
    )(planes, rim, short_filter, long_filter, filter_bias.reshape(1, width))
    columns = lax.all_to_all(send, "ctx", split_axis=0, concat_axis=0, tiled=True)
    consts = [jnp.asarray(table) for table in tables(blocks, rows)]
    conv = pl.pallas_call(
        conv_kernel,
        out_shape=jax.ShapeDtypeStruct((blocks, each, rows), BF16),
        in_specs=[VMEM] * 6,
        out_specs=VMEM,
        scratch_shapes=[
            pltpu.VMEM((blocks * 2 * each, rows), F32),
            pltpu.VMEM((blocks * each, rows), F32),
        ],
        compiler_params=PARAMS,
        name="conv",
    )(columns, *consts)
    conv = lax.all_to_all(conv, "ctx", split_axis=0, concat_axis=0, tiled=True)
    whole = lambda shape: pl.BlockSpec(shape, lambda j: (0,) * len(shape))
    partial = pl.pallas_call(
        mix_kernel,
        grid=(shares,),
        out_shape=jax.ShapeDtypeStruct((shares, rows, cols), BF16),
        in_specs=[
            whole((blocks, each, rows)),
            whole((width, rows)),
            whole((width, rows)),
            pl.BlockSpec((width, cols), lambda j: (0, j)),
        ],
        out_specs=pl.BlockSpec((1, rows, cols), lambda j: (j, 0, 0)),
        scratch_shapes=[pltpu.VMEM((rows, width), BF16)],
        compiler_params=PARAMS,
        name="mix",
    )(conv, query, skip, out_weight)
    partial = lax.all_to_all(partial, "tp", split_axis=0, concat_axis=0, tiled=True)
    return pl.pallas_call(
        sum_kernel,
        out_shape=jax.ShapeDtypeStruct((rows, cols), BF16),
        in_specs=[VMEM],
        out_specs=VMEM,
        compiler_params=PARAMS,
        name="total",
    )(partial)


def solution(mesh):
    in_specs = (P("ctx", None, "tp"), P(None, None, "tp"), P("ctx", "tp"), P("tp"), P("tp", None))
    out_specs = P("ctx", "tp")
    return jax.shard_map(body, mesh=mesh, in_specs=in_specs, out_specs=out_specs, check_vma=False)
```

time: 353 us -> 105 us (0.30)
  waiting for transfers between devices: 186 us -> 0.76 us
  starting transfers between devices: 40.3 us -> 3.94 us
  matrix products: 14.5 us -> 0 us
  between operations: 13.8 us -> 0.05 us
  blocking collectives: 74.6 us -> 83.4 us
  other arithmetic: 8.22 us -> 0 us
  Pallas kernels: 0 us -> 5.34 us
    all_to_all x4 -> x0, waiting for transfers between devices: 150 us -> none  [the longest x1 47.9 us: body(): lax.all_to_all(spec_im, 'ctx', split_axis=0, concat_axis=1, tiled=True)]
    all_to_all x4 -> x0, starting transfers between devices: 36.1 us -> none  [the longest x1 9.61 us: body(): lax.all_to_all(turned_im, 'ctx', split_axis=1, concat_axis=0, tiled=True)]
    reduce_scatter x1 -> x0, waiting for transfers between devices: 35.5 us -> none  [body(): lax.psum_scatter(lax.dot_general(out_weight, gated, (((0,), (1,)), ((), (...]
    dot_general x13 -> x0, matrix products: 14.5 us -> none  [the longest x1 4.36 us: body(): lax.dot_general(out_weight, gated, (((0,), (1,)), ((), ())), preferred_el...]
    unnamed x18 -> x20, local copies, waits for them, and re-layouts: 0.92 us -> 9.94 us
    all_to_all x2 -> x3, blocking collectives: 74.6 us -> 83.4 us  [the longest x1 37.7 us: body(): lax.all_to_all(send, 'ctx', split_axis=0, concat_axis=0, tiled=True)]
    pallas_call x0 -> x4, Pallas kernels: none -> 5.34 us  [the longest x1 2.36 us: body(): pl.pallas_call(mix_kernel, grid=(shares,), out_shape=jax.ShapeDtypeStruct...]
    add x3 -> x0, other arithmetic: 3.95 us -> none  [the longest x1 2.73 us: body(): twisted_re = spec_re * tw_cos + spec_im * tw_sin]
  transfers between devices with their start and end apart: 6 -> 1, of which waited for: 5 -> 1; matrix products, arithmetic and copies ran while one was open for 2% -> 0% of each run, Pallas kernels for 0% -> 0%
where the time goes in v1:
time: 105 us; the launch traced here: 104 us
  blocking collectives  83.4 us (79%)
  local copies, waits for them, and re-layouts  10.7 us (10%)
  Pallas kernels  5.34 us (5%)
  starting transfers between devices  3.94 us (4%)
    all_to_all x1, blocking collectives, body(): lax.all_to_all(send, 'ctx', split_axis=0, concat_axis=0, tiled=True)  37.7 us
    all_to_all x1, blocking collectives, body(): lax.all_to_all(partial, 'tp', split_axis=0, concat_axis=0, tiled=True)  23.3 us
    all_to_all x1, blocking collectives, body(): conv = lax.all_to_all(conv, 'ctx', split_axis=0, concat_axis=0, tiled=True)  22.4 us
    unnamed x20, local copies, waits for them, and re-layouts  9.94 us
    ppermute x1, starting transfers between devices, body(): rim = lax.ppermute(planes[:, rows - 2:], 'ctx', route)  3.94 us
    pallas_call x1, Pallas kernels, body(): pl.pallas_call(mix_kernel, grid=(shares,), out_shape=jax.ShapeDtypeStruct...  2.36 us
  transfers between devices with their start and end apart: 1, of which 1 were waited for; matrix products, arithmetic and copies ran while one was open for 0% of the time, Pallas kernels for 0%

profile of v1, /device:TPU:1, one launch (start us, length us, event | category | flops | bytes accessed | tf_op | source)
XLA Modules:
  0.0 104.1 jit_solution(12520311972824281086)
XLA Ops:
  0.0 0.7 slice.4
  0.8 3.9 %collective-permute-start = (bf16[3,2,512]{2,1,0:T(2,128)(2,1)S(1)}, bf16[3,2,512]{2,1,0:T(2,128)(2,1)S(1)}, u32[]{:S(2)}, u32[]{:S(2)}) collective-permute-start(bf16[3,2,512]{2,1,0:T(2,128)(2,1)S(1)} %slice.4), channel_id=1, source_target_pairs={{0,8},{8,16},{16,24},{24,32},{32,40},{40,48},{48,56},{56,64},{64,7... | collective-permute-start | bytes 18440 | tf_op jit(solution)/shard_map/ppermute | solution.py:130
  4.7 0.8 collective-permute-done.rim
  5.5 0.0 copy-start.1
  5.5 1.0 copy-done.1
  6.5 0.0 copy-start.4
  6.5 0.9 copy-done.4
  7.4 0.0 copy-start.8
  7.4 0.7 copy-done.8
  8.1 0.0 copy-start.9
  8.1 0.7 copy-done.9
  8.8 0.5 short.1
  9.3 37.7 %all_to_all.15.columns = bf16[64,16,128]{2,1,0:T(8,128)(2,1)S(1)} all-to-all(bf16[64,16,128]{2,1,0:T(8,128)(2,1)S(1)} %get-tuple-element.8), channel_id=1, replica_groups=mesh['ctx'=64,'tp'=8] {'ctx'}, dimensions={0} | all-to-all | bytes 524288 | tf_op jit(solution)/shard_map/all_to_all | solution.py:143
  47.0 0.0 copy-start.2
  47.0 1.0 copy-done.2
  48.0 0.0 copy-start.3
  48.0 1.0 copy-done.3
  49.0 0.0 copy-start.5
  49.0 0.8 copy-done.5
  49.8 0.0 copy-start.6
  49.8 0.8 copy-done.6
  50.6 0.0 copy-start.7
  50.6 0.8 copy-done.7
  51.4 1.7 %conv.1 = bf16[64,8,128]{2,1,0:T(8,128)(2,1)S(1)} custom-call(bf16[64,16,128]{2,1,0:T(8,128)(2,1)S(1)} %all_to_all.15.columns, bf16[128,128]{1,0:T(8,128)(2,1)S(1)} %copy-done.7, f32[2,64,128]{2,1,0:T(8,128)S(1)} %copy-done.5, bf16[768,256]{1,0:T(8,128)(2,1)S(1)} %copy-done.3, bf16[768,256]{1,0:T(8,128)(2,1)S(1)} %copy-done.2, bf16[64,384]{1,0:T(8,128)(2,1)S(1)} %copy-done.6), custom_call_target="tpu_custom_call" | custom-call | tf_op jit(solution)/shard_map/conv/pallas_call | solution.py:145
  53.1 22.4 %all_to_all.16.conv = bf16[64,8,128]{2,1,0:T(8,128)(2,1)S(1)} all-to-all(bf16[64,8,128]{2,1,0:T(8,128)(2,1)S(1)} %conv.1), channel_id=1, replica_groups=mesh['ctx'=64,'tp'=8] {'ctx'}, dimensions={0} | all-to-all | bytes 262144 | tf_op jit(solution)/shard_map/all_to_all | solution.py:157
  75.5 0.0 copy-start
  75.5 2.2 %copy-done = bf16[512,4096]{1,0:T(8,128)(2,1)S(1)} copy-done((bf16[512,4096]{1,0:T(8,128)(2,1)S(1)}, bf16[512,4096]{1,0:T(8,128)(2,1)}, u32[]{:S(2)}) %copy-start) | copy-done | bytes 4194328
  77.7 2.4 %mix.1 = bf16[8,128,512]{2,1,0:T(8,128)(2,1)S(1)} custom-call(bf16[64,8,128]{2,1,0:T(8,128)(2,1)S(1)} %all_to_all.16.conv, f32[512,128]{1,0:T(8,128)S(1)} %get-tuple-element.9.query, f32[512,128]{1,0:T(8,128)S(1)} %get-tuple-element.10.skip, bf16[512,4096]{1,0:T(8,128)(2,1)S(1)} %copy-done), custom_call_target="tpu_custom_call" | custom-call | tf_op jit(solution)/shard_map/mix/pallas_call | solution.py:159
  80.0 23.3 %all_to_all.17.parts = bf16[8,128,512]{2,1,0:T(8,128)(2,1)S(1)} all-to-all(bf16[8,128,512]{2,1,0:T(8,128)(2,1)S(1)} %mix.1), channel_id=1, replica_groups=mesh['ctx'=64,'tp'=8] {'tp'}, dimensions={0} | all-to-all | bytes 2097152 | tf_op jit(solution)/shard_map/all_to_all | solution.py:174
  103.3 0.8 total.1
Async XLA Ops:
  0.8 4.7 %collective-permute-start = (bf16[3,2,512]{2,1,0:T(2,128)(2,1)S(1)}, bf16[3,2,512]{2,1,0:T(2,128)(2,1)S(1)}, u32[]{:S(2)}, u32[]{:S(2)}) collective-permute-start(bf16[3,2,512]{2,1,0:T(2,128)(2,1)S(1)} %slice.4), channel_id=1, source_target_pairs={{0,8},{8,16},{16,24},{24,32},{32,40},{40,48},{48,56},{56,64},{64,7... | collective-permute-start | bytes 18440 | tf_op jit(solution)/shard_map/ppermute | solution.py:130
  5.5 1.0 copy-start.1
  6.5 0.9 copy-start.4
  7.4 0.7 copy-start.8
  8.1 0.7 copy-start.9
  47.0 1.0 copy-start.2
  48.0 1.0 copy-start.3
  49.0 0.8 copy-start.5
  49.8 0.8 copy-start.6
  50.6 0.8 copy-start.7
  75.5 2.2 %copy-start = (bf16[512,4096]{1,0:T(8,128)(2,1)S(1)}, bf16[512,4096]{1,0:T(8,128)(2,1)}, u32[]{:S(2)}) copy-start(bf16[512,4096]{1,0:T(8,128)(2,1)} %weight.1) | copy-start | bytes 12582916

commit v2 on v1

--- a/solution.py
+++ b/solution.py
@@ -1,4 +1,3 @@
-import functools
 import math
 
 import jax
@@ -51,6 +50,22 @@
     return high, (value - high.astype(F32)).astype(BF16)
 
 
+def stage_kernel(*refs):
+    count = (len(refs) - 2) // 2
+    filt, sources, columns, targets = refs[0], refs[1 : count], refs[count], refs[count + 1 : 2 * count]
+    landed, sems = refs[2 * count :]
+    load = pltpu.make_async_copy(filt, landed, sems.at[0])
+    load.start()
+    copies = []
+    for i, (source, target) in enumerate(zip(sources, targets)):
+        copies.append(pltpu.make_async_copy(source, target, sems.at[i + 1]))
+        copies[-1].start()
+    load.wait()
+    columns[...] = landed[...].T.reshape(columns.shape).astype(columns.dtype)
+    for copy in copies:
+        copy.wait()
+
+
 def short_kernel(features, rim, taps, filt, bias, send, query, skip):
     row = lax.broadcasted_iota(jnp.int32, features.shape[1:], 0)
 
@@ -63,8 +78,7 @@
 
     gate = stream(1) * stream(2)
     groups, both, rows = send.shape
-    each = both // 2
-    parts = [gate.T.reshape(groups, each, rows), filt[...].T.reshape(groups, each, rows)]
+    parts = [gate.T.reshape(groups, both // 2, rows), filt[...].astype(F32)]
     send[...] = jnp.concatenate(parts, axis=1).astype(send.dtype)
     query[...] = stream(0).T
     skip[...] = (bias[...] * gate).T
@@ -106,13 +120,33 @@
     out[...] = spread[...].reshape(out.shape).astype(out.dtype)
 
 
-def mix_kernel(conv, query, skip, weight, out, gated):
-    @pl.when(pl.program_id(0) == 0)
-    def _():
-        conv_out = conv[...].astype(F32).reshape(query.shape) + skip[...]
-        gated[...] = (query[...] * conv_out).T.astype(BF16)
-
-    out[0] = jnp.dot(gated[...], weight[...], preferred_element_type=F32).astype(out.dtype)
+def gate_kernel(conv, query, skip, gated):
+    conv_out = conv[...].astype(F32).reshape(query.shape) + skip[...]
+    gated[...] = (query[...] * conv_out).T.astype(gated.dtype)
+
+
+def core_columns(y, cols):
+    core = lax.rem(lax.axis_index("tp"), 2)
+    return pl.ds(pl.multiple_of((2 * y + core) * cols, cols), cols)
+
+
+def own_kernel(gated, weight, partial, own, sems):
+    chips, _, cols = partial.shape
+    loads = [
+        pltpu.make_async_copy(weight.at[:, core_columns(y, cols)], own.at[y], sems.at[y]) for y in range(chips)
+    ]
+    for load in loads:
+        load.start()
+    for y in range(chips):
+        loads[y].wait()
+        partial[y] = jnp.dot(gated[...], own[y], preferred_element_type=F32)
+
+
+def both_kernel(gated, weight, partial, out):
+    chips, _, cols = partial.shape
+    for y in range(chips):
+        added = jnp.dot(gated[...], weight[:, core_columns(y, cols)], preferred_element_type=F32)
+        out[y] = (partial[y] + added).astype(out.dtype)
 
 
 def sum_kernel(parts, out):
@@ -123,11 +157,28 @@
     rows, streams, width = features.shape
     blocks = lax.axis_size("ctx")
     shares = lax.axis_size("tp")
+    chips = shares // 2
     each = width // blocks
     cols = out_weight.shape[1] // shares
+    swap = [(i, i ^ 1) for i in range(shares)]
+    other_weight = lax.ppermute(out_weight, "tp", swap)
     planes = jnp.transpose(features, (1, 0, 2))
     route = [(i, i + 1) for i in range(blocks - 1)]
     rim = lax.ppermute(planes[:, rows - 2 :], "ctx", route)
+    consts = [jnp.asarray(table) for table in tables(blocks, rows)]
+    staged = [planes, short_filter, filter_bias.reshape(1, width), *consts]
+    filt, planes, taps, bias, *consts = pl.pallas_call(
+        stage_kernel,
+        out_shape=(
+            jax.ShapeDtypeStruct((blocks, each, rows), BF16),
+            *(jax.ShapeDtypeStruct(array.shape, array.dtype) for array in staged),
+        ),
+        in_specs=[pl.BlockSpec(memory_space=pltpu.HBM)] * (len(staged) + 1),
+        out_specs=(VMEM,) * (len(staged) + 1),
+        scratch_shapes=[pltpu.VMEM((rows, width), F32), pltpu.SemaphoreType.DMA((len(staged) + 1,))],
+        compiler_params=PARAMS,
+        name="stage",
+    )(*(pltpu.with_memory_space_constraint(array, pltpu.HBM) for array in (long_filter, *staged)))
     send, query, skip = pl.pallas_call(
         short_kernel,
         out_shape=(
@@ -139,9 +190,9 @@
         out_specs=(VMEM, VMEM, VMEM),
         compiler_params=PARAMS,
         name="short",
-    )(planes, rim, short_filter, long_filter, filter_bias.reshape(1, width))
+    )(planes, rim, taps, filt, bias)
     columns = lax.all_to_all(send, "ctx", split_axis=0, concat_axis=0, tiled=True)
-    consts = [jnp.asarray(table) for table in tables(blocks, rows)]
+    columns, other_weight = lax.optimization_barrier((columns, other_weight))
     conv = pl.pallas_call(
         conv_kernel,
         out_shape=jax.ShapeDtypeStruct((blocks, each, rows), BF16),
@@ -155,23 +206,36 @@
         name="conv",
     )(columns, *consts)
     conv = lax.all_to_all(conv, "ctx", split_axis=0, concat_axis=0, tiled=True)
-    whole = lambda shape: pl.BlockSpec(shape, lambda j: (0,) * len(shape))
+    gated = pl.pallas_call(
+        gate_kernel,
+        out_shape=jax.ShapeDtypeStruct((rows, width), BF16),
+        in_specs=[VMEM] * 3,
+        out_specs=VMEM,
+        compiler_params=PARAMS,
+        name="gate",
+    )(conv, query, skip)
+    other_gated = lax.ppermute(gated, "tp", swap)
     partial = pl.pallas_call(
-        mix_kernel,
-        grid=(shares,),
-        out_shape=jax.ShapeDtypeStruct((shares, rows, cols), BF16),
-        in_specs=[
-            whole((blocks, each, rows)),
-            whole((width, rows)),
-            whole((width, rows)),
-            pl.BlockSpec((width, cols), lambda j: (0, j)),
-        ],
-        out_specs=pl.BlockSpec((1, rows, cols), lambda j: (j, 0, 0)),
-        scratch_shapes=[pltpu.VMEM((rows, width), BF16)],
-        compiler_params=PARAMS,
-        name="mix",
-    )(conv, query, skip, out_weight)
-    partial = lax.all_to_all(partial, "tp", split_axis=0, concat_axis=0, tiled=True)
+        own_kernel,
+        out_shape=jax.ShapeDtypeStruct((chips, rows, cols), F32),
+        in_specs=[VMEM, pl.BlockSpec(memory_space=pltpu.HBM)],
+        out_specs=VMEM,
+        scratch_shapes=[pltpu.VMEM((chips, width, cols), BF16), pltpu.SemaphoreType.DMA((chips,))],
+        compiler_params=PARAMS,
+        name="own",
+    )(gated, pltpu.with_memory_space_constraint(out_weight, pltpu.HBM))
+    partial = pl.pallas_call(
+        both_kernel,
+        out_shape=jax.ShapeDtypeStruct((chips, rows, cols), BF16),
+        in_specs=[VMEM] * 3,
+        out_specs=VMEM,
+        compiler_params=PARAMS,
+        name="both",
+    )(other_gated, other_weight, partial)
+    columns_of = [[2 * y + core for y in range(chips)] for core in range(2)]
+    partial = lax.all_to_all(
+        partial, "tp", split_axis=0, concat_axis=0, tiled=True, axis_index_groups=columns_of
+    )
     return pl.pallas_call(
         sum_kernel,
         out_shape=jax.ShapeDtypeStruct((rows, cols), BF16),

time: 105 us -> 93.3 us (0.89)
  blocking collectives: 83.4 us -> 69.7 us
  starting transfers between devices: 3.94 us -> 15.3 us
  local copies, waits for them, and re-layouts: 10.7 us -> 0.75 us
  Pallas kernels: 5.34 us -> 7 us
    ppermute x0 -> x2, starting transfers between devices: none -> 14.1 us  [the longest x1 8.78 us: body(): other_weight = lax.ppermute(out_weight, 'tp', swap)]
    all_to_all x1, blocking collectives: 23.3 us -> 13.3 us  [body(): lax.all_to_all(partial, 'tp', split_axis=0, concat_axis=0, tiled=True, ax...]
    unnamed x20 -> x0, local copies, waits for them, and re-layouts: 9.94 us -> none
    all_to_all x1, blocking collectives: 37.7 us -> 34 us  [body(): lax.all_to_all(send, 'ctx', split_axis=0, concat_axis=0, tiled=True)]
    ppermute x1, starting transfers between devices: 3.94 us -> 1.29 us  [body(): rim = lax.ppermute(planes[:, rows - 2:], 'ctx', route)]
    pallas_call x1 -> x4, Pallas kernels: 2.36 us -> 4.1 us  [the longest x1 2.03 us: body(): pl.pallas_call(own_kernel, out_shape=jax.ShapeDtypeStruct((chips, rows, c...]
  transfers between devices with their start and end apart: 1 -> 3, of which waited for: 1 -> 0; matrix products, arithmetic and copies ran while one was open for 0% -> 1% of each run, Pallas kernels for 0% -> 4%
where the time goes in v2:
time: 93.3 us; the launch traced here: 92.9 us
  blocking collectives  69.7 us (75%)
  starting transfers between devices  15.3 us (16%)
  Pallas kernels  7 us (8%)
    all_to_all x1, blocking collectives, body(): lax.all_to_all(send, 'ctx', split_axis=0, concat_axis=0, tiled=True)  34 us
    all_to_all x1, blocking collectives, body(): conv = lax.all_to_all(conv, 'ctx', split_axis=0, concat_axis=0, tiled=True)  22.5 us
    all_to_all x1, blocking collectives, body(): lax.all_to_all(partial, 'tp', split_axis=0, concat_axis=0, tiled=True, ax...  13.3 us
    ppermute x1, starting transfers between devices, body(): other_weight = lax.ppermute(out_weight, 'tp', swap)  8.78 us
    ppermute x1, starting transfers between devices, body(): other_gated = lax.ppermute(gated, 'tp', swap)  5.28 us
    pallas_call x1, Pallas kernels, body(): pl.pallas_call(own_kernel, out_shape=jax.ShapeDtypeStruct((chips, rows, c...  2.03 us
  transfers between devices with their start and end apart: 3, of which 0 were waited for; matrix products, arithmetic and copies ran while one was open for 1% of the time, Pallas kernels for 4%

profile of v2, /device:TPU:1, one launch (start us, length us, event | category | flops | bytes accessed | tf_op | source)
XLA Modules:
  0.0 92.9 jit_solution(14779058917796810867)
XLA Ops:
  0.0 8.8 %collective-permute-start.1 = (bf16[512,4096]{1,0:T(8,128)(2,1)}, bf16[512,4096]{1,0:T(8,128)(2,1)S(1)}, u32[]{:S(2)}, u32[]{:S(2)}) collective-permute-start(bf16[512,4096]{1,0:T(8,128)(2,1)} %weight.1), channel_id=1, source_target_pairs={{0,1},{1,0},{2,3},{3,2},{4,5},{5,4},{6,7},{7,6},{8,9},{9,8},{10,11... | collective-permute-start | bytes 12582920 | tf_op jit(solution)/shard_map/ppermute | solution.py:164
  8.8 0.8 slice.4
  9.5 1.3 %collective-permute-start = (bf16[3,2,512]{2,1,0:T(2,128)(2,1)S(1)}, bf16[3,2,512]{2,1,0:T(2,128)(2,1)S(1)}, u32[]{:S(2)}, u32[]{:S(2)}) collective-permute-start(bf16[3,2,512]{2,1,0:T(2,128)(2,1)S(1)} %slice.4), channel_id=1, source_target_pairs={{0,8},{8,16},{16,24},{24,32},{32,40},{40,48},{48,56},{56,64},{64,7... | collective-permute-start | bytes 18440 | tf_op jit(solution)/shard_map/ppermute | solution.py:167
  10.8 1.5 %stage.1 = (bf16[64,8,128]{2,1,0:T(8,128)(2,1)S(1)}, bf16[3,128,512]{2,1,0:T(8,128)(2,1)S(1)}, f32[3,3,512]{2,1,0:T(4,128)S(1)}, f32[1,512]{1,0:T(1,128)S(1)}, b...) custom-call(f32[128,512]{1,0:T(8,128)} %refs_0_.1, ...), custom_call_target="tpu_custom_call" | custom-call | tf_op jit(solution)/shard_map/stage/pallas_call | solution.py:170
  12.3 0.0 collective-permute-done.rim
  12.3 0.5 short.1
  12.8 34.0 %all_to_all.15.columns = bf16[64,16,128]{2,1,0:T(8,128)(2,1)S(1)} all-to-all(bf16[64,16,128]{2,1,0:T(8,128)(2,1)S(1)} %get-tuple-element.23), channel_id=1, replica_groups=mesh['ctx'=64,'tp'=8] {'ctx'}, dimensions={0} | all-to-all | bytes 524288 | tf_op jit(solution)/shard_map/all_to_all | solution.py:194
  46.8 0.0 collective-permute-done.1.weight
  46.8 1.7 %conv.1 = bf16[64,8,128]{2,1,0:T(8,128)(2,1)S(1)} custom-call(bf16[64,16,128]{2,1,0:T(8,128)(2,1)S(1)} %all_to_all.15.columns, bf16[128,128]{1,0:T(8,128)(2,1)S(1)} %get-tuple-element.25.first, f32[2,64,128]{2,1,0:T(8,128)S(1)} %get-tuple-element.26.twist, bf16[768,256]{1,0:T(8,128)(2,1)S(1)} %get-tuple-element.27.forward, ...), custom_call_target="tpu_custom_call" | custom-call | tf_op jit(solution)/shard_map/conv/pallas_call | solution.py:196
  48.5 22.5 %all_to_all.16.conv = bf16[64,8,128]{2,1,0:T(8,128)(2,1)S(1)} all-to-all(bf16[64,8,128]{2,1,0:T(8,128)(2,1)S(1)} %conv.1), channel_id=1, replica_groups=mesh['ctx'=64,'tp'=8] {'ctx'}, dimensions={0} | all-to-all | bytes 262144 | tf_op jit(solution)/shard_map/all_to_all | solution.py:208
  71.0 0.1 gate.1.gated
  71.1 5.3 %collective-permute-start.2 = (bf16[128,512]{1,0:T(8,128)(2,1)S(1)}, bf16[128,512]{1,0:T(8,128)(2,1)S(1)}, u32[]{:S(2)}, u32[]{:S(2)}) collective-permute-start(bf16[128,512]{1,0:T(8,128)(2,1)S(1)} %gate.1.gated), channel_id=1, source_target_pairs={{0,1},{1,0},{2,3},{3,2},{4,5},{5,4},{6,7},{7,6},{8,9},{9,8},{10,11... | collective-permute-start | bytes 393224 | tf_op jit(solution)/shard_map/ppermute | solution.py:217
  76.4 2.0 %own.1.partial = f32[4,128,512]{2,1,0:T(8,128)S(1)} custom-call(bf16[128,512]{1,0:T(8,128)(2,1)S(1)} %gate.1.gated, bf16[512,4096]{1,0:T(8,128)(2,1)} %weight.1), custom_call_target="tpu_custom_call" | custom-call | tf_op jit(solution)/shard_map/own/pallas_call | solution.py:218
  78.4 0.0 collective-permute-done.2.gated
  78.4 0.5 both.1
  78.9 13.3 %all_to_all.17.parts = bf16[4,128,512]{2,1,0:T(8,128)(2,1)S(1)} all-to-all(bf16[4,128,512]{2,1,0:T(8,128)(2,1)S(1)} %both.1), channel_id=1, replica_groups={{0,2,4,6},{1,3,5,7},{8,10,12,14},{9,11,13,15},{16,18,20,22},{17,19,21,2..., dimensions={0} | all-to-all | bytes 1048576 | tf_op jit(solution)/shard_map/all_to_all | solution.py:236
  92.2 0.7 total.1
Async XLA Ops:
  0.0 46.8 %collective-permute-start.1 = (bf16[512,4096]{1,0:T(8,128)(2,1)}, bf16[512,4096]{1,0:T(8,128)(2,1)S(1)}, u32[]{:S(2)}, u32[]{:S(2)}) collective-permute-start(bf16[512,4096]{1,0:T(8,128)(2,1)} %weight.1), channel_id=1, source_target_pairs={{0,1},{1,0},{2,3},{3,2},{4,5},{5,4},{6,7},{7,6},{8,9},{9,8},{10,11... | collective-permute-start | bytes 12582920 | tf_op jit(solution)/shard_map/ppermute | solution.py:164
  9.5 2.8 %collective-permute-start = (bf16[3,2,512]{2,1,0:T(2,128)(2,1)S(1)}, bf16[3,2,512]{2,1,0:T(2,128)(2,1)S(1)}, u32[]{:S(2)}, u32[]{:S(2)}) collective-permute-start(bf16[3,2,512]{2,1,0:T(2,128)(2,1)S(1)} %slice.4), channel_id=1, source_target_pairs={{0,8},{8,16},{16,24},{24,32},{32,40},{40,48},{48,56},{56,64},{64,7... | collective-permute-start | bytes 18440 | tf_op jit(solution)/shard_map/ppermute | solution.py:167
  71.1 7.3 %collective-permute-start.2 = (bf16[128,512]{1,0:T(8,128)(2,1)S(1)}, bf16[128,512]{1,0:T(8,128)(2,1)S(1)}, u32[]{:S(2)}, u32[]{:S(2)}) collective-permute-start(bf16[128,512]{1,0:T(8,128)(2,1)S(1)} %gate.1.gated), channel_id=1, source_target_pairs={{0,1},{1,0},{2,3},{3,2},{4,5},{5,4},{6,7},{7,6},{8,9},{9,8},{10,11... | collective-permute-start | bytes 393224 | tf_op jit(solution)/shard_map/ppermute | solution.py:217

commit v3 on v2

v3 whole, which is shorter than its diff:
```python
import functools
import math

import jax
import jax.numpy as jnp
import numpy as np
from jax import lax
from jax.experimental import pallas as pl
from jax.experimental.pallas import tpu as pltpu
from jax.sharding import PartitionSpec as P

F32 = jnp.float32
BF16 = jnp.bfloat16
VMEM = pl.BlockSpec(memory_space=pltpu.VMEM)
RIM = 16
PARAMS = pltpu.CompilerParams(vmem_limit_bytes=24 * 1024 * 1024)


def halves(table):
    high = table.astype(BF16)
    low = (table - high.astype(np.float32)).astype(BF16)
    return high, low


def tables(blocks, rows):
    length = blocks * rows
    freq = np.arange(blocks) + 0.25
    outer = 2.0 * math.pi * freq[:, None] * np.arange(blocks)[None, :] / blocks
    first = np.concatenate([np.cos(outer), -np.sin(outer)], axis=0).astype(np.float32)
    last = (np.concatenate([np.cos(outer.T), -np.sin(outer.T)], axis=1) / length).astype(np.float32)
    turn = 2.0 * math.pi * freq[:, None] * np.arange(rows)[None, :] / length
    twist = np.stack([np.cos(turn), np.sin(turn)]).astype(np.float32)
    inner = 2.0 * math.pi * (np.outer(np.arange(rows), np.arange(rows)) % rows) / rows
    cos, sin = np.cos(inner), np.sin(inner)
    forward = np.block([[cos, -sin], [sin, cos]]).astype(np.float32)
    backward = np.block([[cos, sin], [-sin, cos]]).astype(np.float32)
    first_hi, first_lo = halves(first)
    last_hi, last_lo = halves(last)
    forward_hi, forward_lo = halves(forward)
    backward_hi, backward_lo = halves(backward)
    return (
        np.concatenate([first_hi, first_lo], axis=1),
        twist,
        np.concatenate([forward_hi, forward_hi, forward_lo], axis=0),
        np.concatenate([backward_hi, backward_hi, backward_lo], axis=0),
        np.concatenate([last_hi, last_hi, last_lo], axis=1),
    )


def split(value):
    high = value.astype(BF16)
    return high, (value - high.astype(F32)).astype(BF16)


def load_all(sources, targets, sems):
    copies = [
        pltpu.make_async_copy(source, target, sems.at[i])
        for i, (source, target) in enumerate(zip(sources, targets))
    ]
    for copy in copies:
        copy.start()
    return copies


def short_kernel(count, *refs):
    inputs, (send, query, skip), tables = refs[:count], refs[count : count + 3], refs[count + 3 : 2 * count - 1]
    features, taps, filt, bias, wide, corner, sems = refs[2 * count - 1 :]
    copies = load_all(inputs, (features, taps, filt, bias, *tables), sems)
    for copy in copies[:4]:
        copy.wait()
    rows, width = filt.shape
    each = RIM // 2
    groups = width // each
    pitch = send.shape[0] // groups
    row = lax.broadcasted_iota(jnp.int32, (rows, width), 0)

    def stream(j):
        current = features[j].astype(F32)
        one = jnp.where(row == 0, 0.0, pltpu.roll(current, 1, 0))
        two = jnp.where(row < 2, 0.0, pltpu.roll(current, 2, 0))
        near, far = taps[1, j : j + 1], taps[2, j : j + 1]
        after = [near * current[rows - 1 :] + far * current[rows - 2 : rows - 1], far * current[rows - 1 :]]
        return taps[0, j : j + 1] * current + near * one + far * two, after

    asked, asked_after = stream(0)
    key, key_after = stream(1)
    value, value_after = stream(2)
    gate = key * value
    edge = [key[:2], value[:2], asked[:2], *key_after, *value_after, *asked_after, bias[...]]
    edge = jnp.concatenate([*edge, jnp.zeros((rows - 13, width), F32)], axis=0)
    corner[...] = edge.T
    lane = lax.broadcasted_iota(jnp.int32, (groups, rows), 1)
    packed = jnp.zeros((groups, rows), F32)
    for ch in range(each):
        mine = corner[pl.ds(ch, groups, stride=each), :]
        packed += jnp.where(lane // RIM == ch, pltpu.roll(mine, RIM * ch, 1) if ch else mine, 0.0)
    gate_t, filt_t = gate.T, filt[...].T
    for group in range(groups):
        wide[pitch * group : pitch * group + each] = gate_t[each * group : each * (group + 1)]
        wide[pitch * group + each : pitch * group + 2 * each] = filt_t[each * group : each * (group + 1)]
    wide[pl.ds(2 * each, groups, stride=pitch), :] = packed
    wide[pl.ds(2 * each + 1, groups, stride=pitch), :] = jnp.zeros((groups, rows), F32)
    send[...] = wide[...].astype(send.dtype)
    query[...] = asked.T
    skip[...] = (bias[...] * gate).T
    for copy in copies[4:]:
        copy.wait()


def conv_kernel(columns, first, twist, forward, backward, last, out, gathered, spread):
    each, blocks, rows = RIM // 2, out.shape[0], out.shape[2]
    both = 2 * each
    pitch = columns.shape[0] // blocks
    gathered[...] = columns[...].astype(F32)
    edge = gathered[pl.ds(both, blocks, stride=pitch), :]
    before = jnp.where(lax.broadcasted_iota(jnp.int32, edge.shape, 0) == 0, 0.0, pltpu.roll(edge, 1, 0))
    featurized = edge + pltpu.roll(before, rows - 6, 1)
    edge_gate = featurized * pltpu.roll(featurized, rows - 2, 1)
    edge_query = pltpu.roll(featurized, rows - 4, 1)
    edge_skip = pltpu.roll(edge, rows - 12, 1)
    lane = lax.broadcasted_iota(jnp.int32, edge.shape, 1)

    def channel(array, ch):
        return pltpu.roll(array, rows - RIM * ch, 1) if ch else array

    streams = [gathered[pl.ds(ch, blocks, stride=pitch), :] for ch in range(both)]
    for ch in range(each):
        streams[ch] = jnp.where(lane < 2, channel(edge_gate, ch), streams[ch])
    wide = jnp.concatenate(streams, axis=1).astype(BF16)
    outer = jnp.dot(first[...], jnp.concatenate([wide, wide], axis=0), preferred_element_type=F32)
    cos, sin = twist[0], twist[1]
    twisted = []
    for ch in range(both):
        re = outer[:blocks, ch * rows : (ch + 1) * rows]
        im = outer[blocks:, ch * rows : (ch + 1) * rows]
        twisted.append(jnp.concatenate([re * cos + im * sin, im * cos - re * sin], axis=1))
    high, low = split(jnp.concatenate(twisted, axis=0))
    spectrum = jnp.dot(jnp.concatenate([high, low, high], axis=1), forward[...], preferred_element_type=F32)
    gate, filt = spectrum[: each * blocks], spectrum[each * blocks :]
    gate_re, gate_im = gate[:, :rows], gate[:, rows:]
    filt_re, filt_im = filt[:, :rows], filt[:, rows:]
    product = jnp.concatenate(
        [gate_re * filt_re - gate_im * filt_im, gate_re * filt_im + gate_im * filt_re], axis=1
    )
    high, low = split(product)
    inner = jnp.dot(jnp.concatenate([high, low, high], axis=1), backward[...], preferred_element_type=F32)
    turned = []
    for ch in range(each):
        re = inner[ch * blocks : (ch + 1) * blocks, :rows]
        im = inner[ch * blocks : (ch + 1) * blocks, rows:]
        turned.append(jnp.concatenate([re * cos - im * sin, re * sin + im * cos], axis=0))
    high, low = split(jnp.concatenate(turned, axis=1))
    result = jnp.dot(last[...], jnp.concatenate([high, low, high], axis=0), preferred_element_type=F32)
    for ch in range(each):
        part = result[:, ch * rows : (ch + 1) * rows]
        scale = channel(edge_skip, ch)
        scale = jnp.where(lane == 1, pltpu.roll(scale, 1, 1), scale)
        finished = channel(edge_query, ch) * (part + scale * channel(edge_gate, ch))
        spread[pl.ds(ch, blocks, stride=each), :] = jnp.where(lane < 2, finished, part)
    out[...] = spread[...].reshape(out.shape).astype(out.dtype)


def gate_kernel(conv, query, skip, gated):
    arrived = conv[...].astype(F32).reshape(query.shape)
    row = lax.broadcasted_iota(jnp.int32, query.shape, 1)
    finished = jnp.where(row < 2, arrived, query[...] * (arrived + skip[...]))
    gated[...] = finished.T.astype(gated.dtype)


def core_columns(y, cols):
    core = lax.rem(lax.axis_index("tp"), 2)
    return pl.ds(pl.multiple_of((2 * y + core) * cols, cols), cols)


def own_kernel(gated, weight, other, partial, landed, own, sems):
    chips, _, cols = partial.shape
    sources = [array.at[:, core_columns(y, cols)] for array in (weight, other) for y in range(chips)]
    targets = [array.at[y] for array in (own, landed) for y in range(chips)]
    copies = load_all(sources, targets, sems)
    for y in range(chips):
        copies[y].wait()
        partial[y] = jnp.dot(gated[...], own[y], preferred_element_type=F32)
    for copy in copies[chips:]:
        copy.wait()


def both_kernel(gated, weight, partial, out):
    chips, _, cols = partial.shape
    for y in range(chips):
        added = jnp.dot(gated[...], weight[y], preferred_element_type=F32)
        out[y] = (partial[y] + added).astype(out.dtype)


def sum_kernel(parts, out):
    out[...] = jnp.sum(parts[...].astype(F32), axis=0).astype(out.dtype)


def body(features, short_filter, long_filter, filter_bias, out_weight):
    rows, streams, width = features.shape
    blocks = lax.axis_size("ctx")
    shares = lax.axis_size("tp")
    chips = shares // 2
    each = width // blocks
    cols = out_weight.shape[1] // shares
    swap = [(i, i ^ 1) for i in range(shares)]
    other_weight = lax.ppermute(out_weight, "tp", swap)
    consts = [jnp.asarray(table) for table in tables(blocks, rows)]
    planes = jnp.transpose(features, (1, 0, 2))
    staged = [planes, short_filter, long_filter, filter_bias.reshape(1, width), *consts]
    pitch = 2 * each + 2
    send, query, skip, *consts = pl.pallas_call(
        functools.partial(short_kernel, len(staged)),
        out_shape=(
            jax.ShapeDtypeStruct((blocks * pitch, rows), BF16),
            jax.ShapeDtypeStruct((width, rows), F32),
            jax.ShapeDtypeStruct((width, rows), F32),
            *(jax.ShapeDtypeStruct(array.shape, array.dtype) for array in consts),
        ),
        in_specs=[pl.BlockSpec(memory_space=pltpu.HBM)] * len(staged),
        out_specs=(VMEM,) * (3 + len(consts)),
        scratch_shapes=[
            *(pltpu.VMEM(array.shape, array.dtype) for array in staged[:4]),
            pltpu.VMEM((blocks * pitch, rows), F32),
            pltpu.VMEM((width, rows), F32),
            pltpu.SemaphoreType.DMA((len(staged),)),
        ],
        compiler_params=PARAMS,
        name="short",
    )(*(pltpu.with_memory_space_constraint(array, pltpu.HBM) for array in staged))
    send = send.reshape(blocks, pitch // 2, 2, rows)
    columns = lax.all_to_all(send, "ctx", split_axis=0, concat_axis=0, tiled=True)
    columns = columns.reshape(blocks * pitch, rows)
    columns, other_weight = lax.optimization_barrier((columns, other_weight))
    conv = pl.pallas_call(
        conv_kernel,
        out_shape=jax.ShapeDtypeStruct((blocks, each, rows), BF16),
        in_specs=[VMEM] * 6,
        out_specs=VMEM,
        scratch_shapes=[
            pltpu.VMEM((blocks * pitch, rows), F32),
            pltpu.VMEM((blocks * each, rows), F32),
        ],
        compiler_params=PARAMS,
        name="conv",
    )(columns, *consts)
    conv = lax.all_to_all(conv, "ctx", split_axis=0, concat_axis=0, tiled=True)
    gated = pl.pallas_call(
        gate_kernel,
        out_shape=jax.ShapeDtypeStruct((rows, width), BF16),
        in_specs=[VMEM] * 3,
        out_specs=VMEM,
        compiler_params=PARAMS,
        name="gate",
    )(conv, query, skip)
    other_gated = lax.ppermute(gated, "tp", swap)
    partial, landed = pl.pallas_call(
        own_kernel,
        out_shape=(
            jax.ShapeDtypeStruct((chips, rows, cols), F32),
            jax.ShapeDtypeStruct((chips, width, cols), BF16),
        ),
        in_specs=[VMEM] + [pl.BlockSpec(memory_space=pltpu.HBM)] * 2,
        out_specs=(VMEM, VMEM),
        scratch_shapes=[pltpu.VMEM((chips, width, cols), BF16), pltpu.SemaphoreType.DMA((2 * chips,))],
        compiler_params=PARAMS,
        name="own",
    )(gated, *(pltpu.with_memory_space_constraint(array, pltpu.HBM) for array in (out_weight, other_weight)))
    partial = pl.pallas_call(
        both_kernel,
        out_shape=jax.ShapeDtypeStruct((chips, rows, cols), BF16),
        in_specs=[VMEM] * 3,
        out_specs=VMEM,
        compiler_params=PARAMS,
        name="both",
    )(other_gated, landed, partial)
    columns_of = [[2 * y + core for y in range(chips)] for core in range(2)]
    partial = lax.all_to_all(
        partial, "tp", split_axis=0, concat_axis=0, tiled=True, axis_index_groups=columns_of
    )
    return pl.pallas_call(
        sum_kernel,
        out_shape=jax.ShapeDtypeStruct((rows, cols), BF16),
        in_specs=[VMEM],
        out_specs=VMEM,
        compiler_params=PARAMS,
        name="total",
    )(partial)


def solution(mesh):
    in_specs = (P("ctx", None, "tp"), P(None, None, "tp"), P("ctx", "tp"), P("tp"), P("tp", None))
    out_specs = P("ctx", "tp")
    return jax.shard_map(body, mesh=mesh, in_specs=in_specs, out_specs=out_specs, check_vma=False)
```

time: 93.3 us -> 90.9 us (0.974)
  starting transfers between devices: 15.3 us -> 14.3 us
    all_to_all x1, blocking collectives: 22.5 us -> 21 us  [body(): conv = lax.all_to_all(conv, 'ctx', split_axis=0, concat_axis=0, tiled=True)]
    ppermute x1 -> x0, starting transfers between devices: 1.29 us -> none  [body(): rim = lax.ppermute(planes[:, rows - 2:], 'ctx', route)]
    pallas_call x3 -> x2, Pallas kernels: 3.97 us -> 4.14 us  [the longest x1 2.26 us: body(): pl.pallas_call(own_kernel, out_shape=(jax.ShapeDtypeStruct((chips, rows,...]
  transfers between devices with their start and end apart: 3 -> 2, of which waited for: 0 -> 0; matrix products, arithmetic and copies ran while one was open for 1% -> 0% of each run, Pallas kernels for 4% -> 5%
where the time goes in v3:
time: 90.9 us; the launch traced here: 90.6 us
  blocking collectives  69 us (76%)
  starting transfers between devices  14.3 us (16%)
  Pallas kernels  7.32 us (8%)
    all_to_all x1, blocking collectives, body(): lax.all_to_all(send, 'ctx', split_axis=0, concat_axis=0, tiled=True)  34.6 us
    all_to_all x1, blocking collectives, body(): conv = lax.all_to_all(conv, 'ctx', split_axis=0, concat_axis=0, tiled=True)  21 us
    all_to_all x1, blocking collectives, body(): lax.all_to_all(partial, 'tp', split_axis=0, concat_axis=0, tiled=True, ax...  13.3 us
    ppermute x1, starting transfers between devices, body(): other_weight = lax.ppermute(out_weight, 'tp', swap)  8.78 us
    ppermute x1, starting transfers between devices, body(): other_gated = lax.ppermute(gated, 'tp', swap)  5.51 us
    pallas_call x1, Pallas kernels, body(): pl.pallas_call(own_kernel, out_shape=(jax.ShapeDtypeStruct((chips, rows,...  2.26 us
    pallas_call x1, Pallas kernels, body(): pl.pallas_call(conv_kernel, out_shape=jax.ShapeDtypeStruct((blocks, each,...  1.91 us
    pallas_call x1, Pallas kernels, body(): pl.pallas_call(functools.partial(short_kernel, len(staged)), out_shape=(j...  1.88 us
  transfers between devices with their start and end apart: 2, of which 0 were waited for; matrix products, arithmetic and copies ran while one was open for 0% of the time, Pallas kernels for 5%

profile of v3, /device:TPU:1, one launch (start us, length us, event | category | flops | bytes accessed | tf_op | source)
XLA Modules:
  0.0 90.6 jit_solution(6013763841502081895)
XLA Ops:
  0.0 8.8 %collective-permute-start = (bf16[512,4096]{1,0:T(8,128)(2,1)}, bf16[512,4096]{1,0:T(8,128)(2,1)S(1)}, u32[]{:S(2)}, u32[]{:S(2)}) collective-permute-start(bf16[512,4096]{1,0:T(8,128)(2,1)} %weight.1), channel_id=1, source_target_pairs={{0,1},{1,0},{2,3},{3,2},{4,5},{5,4},{6,7},{7,6},{8,9},{9,8},{10,11... | collective-permute-start | bytes 12582920 | tf_op jit(solution)/shard_map/ppermute | solution.py:206
  8.8 1.9 %short.1 = (bf16[1152,128]{1,0:T(8,128)(2,1)S(1)}, f32[512,128]{1,0:T(8,128)S(1)}, f32[512,128]{1,0:T(8,128)S(1)}, bf16[128,128]{1,0:T(8,128)(2,1)S(1)}, f32[2,6...) custom-call(bf16[3,128,512]{2,1,0:T(8,128)(2,1)} %bitcast.6, ...), custom_call_target="tpu_custom_call" | custom-call | tf_op jit(solution)/shard_map/short/pallas_call | solution.py:211
  10.7 34.6 %all_to_all.15 = bf16[64,9,2,128]{3,2,1,0:T(2,128)(2,1)S(1)} all-to-all(bf16[64,9,2,128]{3,2,1,0:T(2,128)(2,1)S(1)} %bitcast.5), channel_id=1, replica_groups=mesh['ctx'=64,'tp'=8] {'ctx'}, dimensions={0} | all-to-all | bytes 589824 | tf_op jit(solution)/shard_map/all_to_all | solution.py:231
  45.3 0.0 collective-permute-done.other
  45.3 0.0 copy-start
  45.3 1.9 %conv.1 = bf16[64,8,128]{2,1,0:T(8,128)(2,1)S(1)} custom-call(bf16[1152,128]{1,0:T(8,128)(2,1)S(1)} %bitcast.4, bf16[128,128]{1,0:T(8,128)(2,1)S(1)} %get-tuple-element.19.first, f32[2,64,128]{2,1,0:T(8,128)S(1)} %get-tuple-element.20.twist, bf16[768,256]{1,0:T(8,128)(2,1)S(1)} %get-tuple-element.21.forward, ...), custom_call_target="tpu_custom_call" | custom-call | tf_op jit(solution)/shard_map/conv/pallas_call | solution.py:234
  47.2 21.0 %all_to_all.16.conv = bf16[64,8,128]{2,1,0:T(8,128)(2,1)S(1)} all-to-all(bf16[64,8,128]{2,1,0:T(8,128)(2,1)S(1)} %conv.1), channel_id=1, replica_groups=mesh['ctx'=64,'tp'=8] {'ctx'}, dimensions={0} | all-to-all | bytes 262144 | tf_op jit(solution)/shard_map/all_to_all | solution.py:246
  68.2 0.1 gate.1.gated
  68.4 5.5 %collective-permute-start.1 = (bf16[128,512]{1,0:T(8,128)(2,1)S(1)}, bf16[128,512]{1,0:T(8,128)(2,1)S(1)}, u32[]{:S(2)}, u32[]{:S(2)}) collective-permute-start(bf16[128,512]{1,0:T(8,128)(2,1)S(1)} %gate.1.gated), channel_id=1, source_target_pairs={{0,1},{1,0},{2,3},{3,2},{4,5},{5,4},{6,7},{7,6},{8,9},{9,8},{10,11... | collective-permute-start | bytes 393224 | tf_op jit(solution)/shard_map/ppermute | solution.py:255
  73.9 0.0 copy-done
  73.9 2.3 %own.1 = (f32[4,128,512]{2,1,0:T(8,128)S(1)}, bf16[4,512,512]{2,1,0:T(8,128)(2,1)S(1)}) custom-call(bf16[128,512]{1,0:T(8,128)(2,1)S(1)} %gate.1.gated, bf16[512,4096]{1,0:T(8,128)(2,1)} %weight.1, bf16[512,4096]{1,0:T(8,128)(2,1)} %copy-done), custom_call_target="tpu_custom_call" | custom-call | tf_op jit(solution)/shard_map/own/pallas_call | solution.py:256
  76.2 0.0 collective-permute-done.1.gated
  76.2 0.4 both.1
  76.6 13.3 %all_to_all.17.parts = bf16[4,128,512]{2,1,0:T(8,128)(2,1)S(1)} all-to-all(bf16[4,128,512]{2,1,0:T(8,128)(2,1)S(1)} %both.1), channel_id=1, replica_groups={{0,2,4,6},{1,3,5,7},{8,10,12,14},{9,11,13,15},{16,18,20,22},{17,19,21,2..., dimensions={0} | all-to-all | bytes 1048576 | tf_op jit(solution)/shard_map/all_to_all | solution.py:277
  89.9 0.7 total.1
Async XLA Ops:
  0.0 45.3 %collective-permute-start = (bf16[512,4096]{1,0:T(8,128)(2,1)}, bf16[512,4096]{1,0:T(8,128)(2,1)S(1)}, u32[]{:S(2)}, u32[]{:S(2)}) collective-permute-start(bf16[512,4096]{1,0:T(8,128)(2,1)} %weight.1), channel_id=1, source_target_pairs={{0,1},{1,0},{2,3},{3,2},{4,5},{5,4},{6,7},{7,6},{8,9},{9,8},{10,11... | collective-permute-start | bytes 12582920 | tf_op jit(solution)/shard_map/ppermute | solution.py:206
  45.3 28.6 %copy-start = (bf16[512,4096]{1,0:T(8,128)(2,1)}, bf16[512,4096]{1,0:T(8,128)(2,1)S(1)}, u32[]{:S(2)}) copy-start(bf16[512,4096]{1,0:T(8,128)(2,1)S(1)} %collective-permute-done.other) | copy-start | bytes 12582916
  68.4 7.8 %collective-permute-start.1 = (bf16[128,512]{1,0:T(8,128)(2,1)S(1)}, bf16[128,512]{1,0:T(8,128)(2,1)S(1)}, u32[]{:S(2)}, u32[]{:S(2)}) collective-permute-start(bf16[128,512]{1,0:T(8,128)(2,1)S(1)} %gate.1.gated), channel_id=1, source_target_pairs={{0,1},{1,0},{2,3},{3,2},{4,5},{5,4},{6,7},{7,6},{8,9},{9,8},{10,11... | collective-permute-start | bytes 393224 | tf_op jit(solution)/shard_map/ppermute | solution.py:255

commit v4 on v3

--- a/solution.py
+++ b/solution.py
@@ -62,10 +62,19 @@
     return copies
 
 
+def columns_of_core(weight, chips, partner):
+    cols = weight.shape[1] // (2 * chips)
+    core = lax.rem(lax.axis_index("tp") + partner, 2)
+    return [weight.at[:, pl.ds(pl.multiple_of((2 * y + core) * cols, cols), cols)] for y in range(chips)]
+
+
 def short_kernel(count, *refs):
-    inputs, (send, query, skip), tables = refs[:count], refs[count : count + 3], refs[count + 3 : 2 * count - 1]
+    inputs, weight = refs[: count - 1], refs[count - 1]
+    (send, query, skip, held), tables = refs[count : count + 4], refs[count + 4 : 2 * count - 1]
     features, taps, filt, bias, wide, corner, sems = refs[2 * count - 1 :]
-    copies = load_all(inputs, (features, taps, filt, bias, *tables), sems)
+    chips = held.shape[0]
+    sources = [*inputs, *columns_of_core(weight, chips, 1)]
+    copies = load_all(sources, (features, taps, filt, bias, *tables, *(held.at[y] for y in range(chips))), sems)
     for copy in copies[:4]:
         copy.wait()
     rows, width = filt.shape
@@ -160,35 +169,25 @@
     out[...] = spread[...].reshape(out.shape).astype(out.dtype)
 
 
-def gate_kernel(conv, query, skip, gated):
+def give_kernel(conv, query, skip, weight, gated, given):
     arrived = conv[...].astype(F32).reshape(query.shape)
     row = lax.broadcasted_iota(jnp.int32, query.shape, 1)
     finished = jnp.where(row < 2, arrived, query[...] * (arrived + skip[...]))
     gated[...] = finished.T.astype(gated.dtype)
-
-
-def core_columns(y, cols):
-    core = lax.rem(lax.axis_index("tp"), 2)
-    return pl.ds(pl.multiple_of((2 * y + core) * cols, cols), cols)
-
-
-def own_kernel(gated, weight, other, partial, landed, own, sems):
-    chips, _, cols = partial.shape
-    sources = [array.at[:, core_columns(y, cols)] for array in (weight, other) for y in range(chips)]
-    targets = [array.at[y] for array in (own, landed) for y in range(chips)]
-    copies = load_all(sources, targets, sems)
+    for y in range(given.shape[0]):
+        given[y] = jnp.dot(gated[...], weight[y], preferred_element_type=F32).astype(given.dtype)
+
+
+def keep_kernel(gated, weight, kept, held, sems):
+    chips = kept.shape[0]
+    copies = load_all(columns_of_core(weight, chips, 0), [held.at[y] for y in range(chips)], sems)
     for y in range(chips):
         copies[y].wait()
-        partial[y] = jnp.dot(gated[...], own[y], preferred_element_type=F32)
-    for copy in copies[chips:]:
-        copy.wait()
-
-
-def both_kernel(gated, weight, partial, out):
-    chips, _, cols = partial.shape
-    for y in range(chips):
-        added = jnp.dot(gated[...], weight[y], preferred_element_type=F32)
-        out[y] = (partial[y] + added).astype(out.dtype)
+        kept[y] = jnp.dot(gated[...], held[y], preferred_element_type=F32)
+
+
+def pair_kernel(kept, arrived, out):
+    out[...] = (kept[...] + arrived[...].astype(F32)).astype(out.dtype)
 
 
 def sum_kernel(parts, out):
@@ -202,27 +201,26 @@
     chips = shares // 2
     each = width // blocks
     cols = out_weight.shape[1] // shares
-    swap = [(i, i ^ 1) for i in range(shares)]
-    other_weight = lax.ppermute(out_weight, "tp", swap)
     consts = [jnp.asarray(table) for table in tables(blocks, rows)]
     planes = jnp.transpose(features, (1, 0, 2))
-    staged = [planes, short_filter, long_filter, filter_bias.reshape(1, width), *consts]
+    staged = [planes, short_filter, long_filter, filter_bias.reshape(1, width), *consts, out_weight]
     pitch = 2 * each + 2
-    send, query, skip, *consts = pl.pallas_call(
+    send, query, skip, held, *consts = pl.pallas_call(
         functools.partial(short_kernel, len(staged)),
         out_shape=(
             jax.ShapeDtypeStruct((blocks * pitch, rows), BF16),
             jax.ShapeDtypeStruct((width, rows), F32),
             jax.ShapeDtypeStruct((width, rows), F32),
+            jax.ShapeDtypeStruct((chips, width, cols), BF16),
             *(jax.ShapeDtypeStruct(array.shape, array.dtype) for array in consts),
         ),
         in_specs=[pl.BlockSpec(memory_space=pltpu.HBM)] * len(staged),
-        out_specs=(VMEM,) * (3 + len(consts)),
+        out_specs=(VMEM,) * (4 + len(consts)),
         scratch_shapes=[
             *(pltpu.VMEM(array.shape, array.dtype) for array in staged[:4]),
             pltpu.VMEM((blocks * pitch, rows), F32),
             pltpu.VMEM((width, rows), F32),
-            pltpu.SemaphoreType.DMA((len(staged),)),
+            pltpu.SemaphoreType.DMA((len(staged) - 1 + chips,)),
         ],
         compiler_params=PARAMS,
         name="short",
@@ -230,7 +228,6 @@
     send = send.reshape(blocks, pitch // 2, 2, rows)
     columns = lax.all_to_all(send, "ctx", split_axis=0, concat_axis=0, tiled=True)
     columns = columns.reshape(blocks * pitch, rows)
-    columns, other_weight = lax.optimization_barrier((columns, other_weight))
     conv = pl.pallas_call(
         conv_kernel,
         out_shape=jax.ShapeDtypeStruct((blocks, each, rows), BF16),
@@ -244,35 +241,35 @@
         name="conv",
     )(columns, *consts)
     conv = lax.all_to_all(conv, "ctx", split_axis=0, concat_axis=0, tiled=True)
-    gated = pl.pallas_call(
-        gate_kernel,
-        out_shape=jax.ShapeDtypeStruct((rows, width), BF16),
-        in_specs=[VMEM] * 3,
-        out_specs=VMEM,
-        compiler_params=PARAMS,
-        name="gate",
-    )(conv, query, skip)
-    other_gated = lax.ppermute(gated, "tp", swap)
-    partial, landed = pl.pallas_call(
-        own_kernel,
+    gated, given = pl.pallas_call(
+        give_kernel,
         out_shape=(
-            jax.ShapeDtypeStruct((chips, rows, cols), F32),
-            jax.ShapeDtypeStruct((chips, width, cols), BF16),
+            jax.ShapeDtypeStruct((rows, width), BF16),
+            jax.ShapeDtypeStruct((chips, rows, cols), BF16),
         ),
-        in_specs=[VMEM] + [pl.BlockSpec(memory_space=pltpu.HBM)] * 2,
+        in_specs=[VMEM] * 4,
         out_specs=(VMEM, VMEM),
-        scratch_shapes=[pltpu.VMEM((chips, width, cols), BF16), pltpu.SemaphoreType.DMA((2 * chips,))],
-        compiler_params=PARAMS,
-        name="own",
-    )(gated, *(pltpu.with_memory_space_constraint(array, pltpu.HBM) for array in (out_weight, other_weight)))
+        compiler_params=PARAMS,
+        name="give",
+    )(conv, query, skip, held)
+    arrived = lax.ppermute(given, "tp", [(i, i ^ 1) for i in range(shares)])
+    kept = pl.pallas_call(
+        keep_kernel,
+        out_shape=jax.ShapeDtypeStruct((chips, rows, cols), F32),
+        in_specs=[VMEM, pl.BlockSpec(memory_space=pltpu.HBM)],
+        out_specs=VMEM,
+        scratch_shapes=[pltpu.VMEM((chips, width, cols), BF16), pltpu.SemaphoreType.DMA((chips,))],
+        compiler_params=PARAMS,
+        name="keep",
+    )(gated, pltpu.with_memory_space_constraint(out_weight, pltpu.HBM))
     partial = pl.pallas_call(
-        both_kernel,
+        pair_kernel,
         out_shape=jax.ShapeDtypeStruct((chips, rows, cols), BF16),
-        in_specs=[VMEM] * 3,
-        out_specs=VMEM,
-        compiler_params=PARAMS,
-        name="both",
-    )(other_gated, landed, partial)
+        in_specs=[VMEM] * 2,
+        out_specs=VMEM,
+        compiler_params=PARAMS,
+        name="pair",
+    )(kept, arrived)
     columns_of = [[2 * y + core for y in range(chips)] for core in range(2)]
     partial = lax.all_to_all(
         partial, "tp", split_axis=0, concat_axis=0, tiled=True, axis_index_groups=columns_of

time: 90.9 us -> 88.2 us (0.970)
  starting transfers between devices: 14.3 us -> 5.55 us
  blocking collectives: 69 us -> 75 us
    ppermute x2 -> x1, starting transfers between devices: 14.3 us -> 5.55 us  [body(): arrived = lax.ppermute(given, 'tp', [(i, i ^ 1) for i in range(shares)])]
    all_to_all x1, blocking collectives: 34.6 us -> 39.4 us  [body(): lax.all_to_all(send, 'ctx', split_axis=0, concat_axis=0, tiled=True)]
    all_to_all x1, blocking collectives: 21 us -> 22.3 us  [body(): conv = lax.all_to_all(conv, 'ctx', split_axis=0, concat_axis=0, tiled=True)]
  transfers between devices with their start and end apart: 2 -> 1, of which waited for: 0 -> 0; matrix products, arithmetic and copies ran while one was open for 0% -> 0% of each run, Pallas kernels for 5% -> 2%
where the time goes in v4:
time: 88.2 us; the launch traced here: 88 us
  blocking collectives  75 us (85%)
  Pallas kernels  7.39 us (8%)
  starting transfers between devices  5.55 us (6%)
    all_to_all x1, blocking collectives, body(): lax.all_to_all(send, 'ctx', split_axis=0, concat_axis=0, tiled=True)  39.4 us
    all_to_all x1, blocking collectives, body(): conv = lax.all_to_all(conv, 'ctx', split_axis=0, concat_axis=0, tiled=True)  22.3 us
    all_to_all x1, blocking collectives, body(): lax.all_to_all(partial, 'tp', split_axis=0, concat_axis=0, tiled=True, ax...  13.3 us
    ppermute x1, starting transfers between devices, body(): arrived = lax.ppermute(given, 'tp', [(i, i ^ 1) for i in range(shares)])  5.55 us
    pallas_call x1, Pallas kernels, body(): pl.pallas_call(functools.partial(short_kernel, len(staged)), out_shape=(j...  2.16 us
    pallas_call x1, Pallas kernels, body(): pl.pallas_call(keep_kernel, out_shape=jax.ShapeDtypeStruct((chips, rows,...  2.03 us
    pallas_call x1, Pallas kernels, body(): pl.pallas_call(conv_kernel, out_shape=jax.ShapeDtypeStruct((blocks, each,...  1.91 us
  transfers between devices with their start and end apart: 1, of which 0 were waited for; matrix products, arithmetic and copies ran while one was open for 0% of the time, Pallas kernels for 2%

profile of v4, /device:TPU:1, one launch (start us, length us, event | category | flops | bytes accessed | tf_op | source)
XLA Modules:
  0.0 88.0 jit_solution(1256892127050276094)
XLA Ops:
  0.0 2.2 %short.1 = (bf16[1152,128]{1,0:T(8,128)(2,1)S(1)}, f32[512,128]{1,0:T(8,128)S(1)}, f32[512,128]{1,0:T(8,128)S(1)}, bf16[4,512,512]{2,1,0:T(8,128)(2,1)S(1)}, bf1...) custom-call(bf16[3,128,512]{2,1,0:T(8,128)(2,1)} %bitcast.6, ...), custom_call_target="tpu_custom_call" | custom-call | tf_op jit(solution)/shard_map/short/pallas_call | solution.py:208
  2.2 39.4 %all_to_all.15 = bf16[64,9,2,128]{3,2,1,0:T(2,128)(2,1)S(1)} all-to-all(bf16[64,9,2,128]{3,2,1,0:T(2,128)(2,1)S(1)} %bitcast.5), channel_id=1, replica_groups=mesh['ctx'=64,'tp'=8] {'ctx'}, dimensions={0} | all-to-all | bytes 589824 | tf_op jit(solution)/shard_map/all_to_all | solution.py:229
  41.6 1.9 %conv.1 = bf16[64,8,128]{2,1,0:T(8,128)(2,1)S(1)} custom-call(bf16[1152,128]{1,0:T(8,128)(2,1)S(1)} %bitcast.4, bf16[128,128]{1,0:T(8,128)(2,1)S(1)} %get-tuple-element.17.first, f32[2,64,128]{2,1,0:T(8,128)S(1)} %get-tuple-element.18.twist, bf16[768,256]{1,0:T(8,128)(2,1)S(1)} %get-tuple-element.19.forward, ...), custom_call_target="tpu_custom_call" | custom-call | tf_op jit(solution)/shard_map/conv/pallas_call | solution.py:231
  43.5 22.3 %all_to_all.16.conv = bf16[64,8,128]{2,1,0:T(8,128)(2,1)S(1)} all-to-all(bf16[64,8,128]{2,1,0:T(8,128)(2,1)S(1)} %conv.1), channel_id=1, replica_groups=mesh['ctx'=64,'tp'=8] {'ctx'}, dimensions={0} | all-to-all | bytes 262144 | tf_op jit(solution)/shard_map/all_to_all | solution.py:243
  65.7 0.5 give.1
  66.2 5.5 %collective-permute-start = (bf16[4,128,512]{2,1,0:T(8,128)(2,1)S(1)}, bf16[4,128,512]{2,1,0:T(8,128)(2,1)S(1)}, u32[]{:S(2)}, u32[]{:S(2)}) collective-permute-start(bf16[4,128,512]{2,1,0:T(8,128)(2,1)S(1)} %get-tuple-element.26), channel_id=1, source_target_pairs={{0,1},{1,0},{2,3},{3,2},{4,5},{5,4},{6,7},{7,6},{8,9},{9,8},{10,11... | collective-permute-start | bytes 1572872 | tf_op jit(solution)/shard_map/ppermute | solution.py:255
  71.8 2.0 %keep.1.kept = f32[4,128,512]{2,1,0:T(8,128)S(1)} custom-call(bf16[128,512]{1,0:T(8,128)(2,1)S(1)} %get-tuple-element.25.gated, bf16[512,4096]{1,0:T(8,128)(2,1)} %weight.1), custom_call_target="tpu_custom_call" | custom-call | tf_op jit(solution)/shard_map/keep/pallas_call | solution.py:256
  73.8 0.0 collective-permute-done.arrived
  73.8 0.1 pair.1
  73.9 13.3 %all_to_all.17.parts = bf16[4,128,512]{2,1,0:T(8,128)(2,1)S(1)} all-to-all(bf16[4,128,512]{2,1,0:T(8,128)(2,1)S(1)} %pair.1), channel_id=1, replica_groups={{0,2,4,6},{1,3,5,7},{8,10,12,14},{9,11,13,15},{16,18,20,22},{17,19,21,2..., dimensions={0} | all-to-all | bytes 1048576 | tf_op jit(solution)/shard_map/all_to_all | solution.py:274
  87.2 0.7 total.1
Async XLA Ops:
  66.2 7.6 %collective-permute-start = (bf16[4,128,512]{2,1,0:T(8,128)(2,1)S(1)}, bf16[4,128,512]{2,1,0:T(8,128)(2,1)S(1)}, u32[]{:S(2)}, u32[]{:S(2)}) collective-permute-start(bf16[4,128,512]{2,1,0:T(8,128)(2,1)S(1)} %get-tuple-element.26), channel_id=1, source_target_pairs={{0,1},{1,0},{2,3},{3,2},{4,5},{5,4},{6,7},{7,6},{8,9},{9,8},{10,11... | collective-permute-start | bytes 1572872 | tf_op jit(solution)/shard_map/ppermute | solution.py:255

commit v5 on v4

--- a/solution.py
+++ b/solution.py
@@ -13,6 +13,7 @@
 BF16 = jnp.bfloat16
 VMEM = pl.BlockSpec(memory_space=pltpu.VMEM)
 RIM = 16
+SIDE = 4
 PARAMS = pltpu.CompilerParams(vmem_limit_bytes=24 * 1024 * 1024)
 
 
@@ -22,10 +23,14 @@
     return high, low
 
 
+def block_order(blocks):
+    return np.arange(blocks).reshape(-1, SIDE).T.reshape(-1)
+
+
 def tables(blocks, rows):
     length = blocks * rows
     freq = np.arange(blocks) + 0.25
-    outer = 2.0 * math.pi * freq[:, None] * np.arange(blocks)[None, :] / blocks
+    outer = 2.0 * math.pi * freq[:, None] * block_order(blocks)[None, :] / blocks
     first = np.concatenate([np.cos(outer), -np.sin(outer)], axis=0).astype(np.float32)
     last = (np.concatenate([np.cos(outer.T), -np.sin(outer.T)], axis=1) / length).astype(np.float32)
     turn = 2.0 * math.pi * freq[:, None] * np.arange(rows)[None, :] / length
@@ -33,18 +38,22 @@
     inner = 2.0 * math.pi * (np.outer(np.arange(rows), np.arange(rows)) % rows) / rows
     cos, sin = np.cos(inner), np.sin(inner)
     forward = np.block([[cos, -sin], [sin, cos]]).astype(np.float32)
-    backward = np.block([[cos, sin], [-sin, cos]]).astype(np.float32)
     first_hi, first_lo = halves(first)
     last_hi, last_lo = halves(last)
     forward_hi, forward_lo = halves(forward)
-    backward_hi, backward_lo = halves(backward)
     return (
         np.concatenate([first_hi, first_lo], axis=1),
         twist,
-        np.concatenate([forward_hi, forward_hi, forward_lo], axis=0),
-        np.concatenate([backward_hi, backward_hi, backward_lo], axis=0),
+        np.stack([forward_hi, forward_lo]),
         np.concatenate([last_hi, last_hi, last_lo], axis=1),
     )
+
+
+def transform(value, matrix):
+    high, low = split(value)
+    total = jnp.dot(high, matrix[0], preferred_element_type=F32)
+    total += jnp.dot(low, matrix[0], preferred_element_type=F32)
+    return total + jnp.dot(high, matrix[1], preferred_element_type=F32)
 
 
 def split(value):
@@ -95,9 +104,9 @@
     key, key_after = stream(1)
     value, value_after = stream(2)
     gate = key * value
-    edge = [key[:2], value[:2], asked[:2], *key_after, *value_after, *asked_after, bias[...]]
-    edge = jnp.concatenate([*edge, jnp.zeros((rows - 13, width), F32)], axis=0)
-    corner[...] = edge.T
+    edge = [key[:2], value[:2], asked[:2], *key_after, *value_after, *asked_after, bias[...], bias[...]]
+    edge = jnp.concatenate([*edge, jnp.zeros((RIM - 14, width), F32)], axis=0)
+    corner[:, :RIM] = edge.T
     lane = lax.broadcasted_iota(jnp.int32, (groups, rows), 1)
     packed = jnp.zeros((groups, rows), F32)
     for ch in range(each):
@@ -110,23 +119,26 @@
     wide[pl.ds(2 * each, groups, stride=pitch), :] = packed
     wide[pl.ds(2 * each + 1, groups, stride=pitch), :] = jnp.zeros((groups, rows), F32)
     send[...] = wide[...].astype(send.dtype)
-    query[...] = asked.T
-    skip[...] = (bias[...] * gate).T
+    query[...] = asked
+    skip[...] = bias[...] * gate
     for copy in copies[4:]:
         copy.wait()
 
 
-def conv_kernel(columns, first, twist, forward, backward, last, out, gathered, spread):
+def conv_kernel(columns, first, twist, forward, last, out, gathered, spread):
     each, blocks, rows = RIM // 2, out.shape[0], out.shape[2]
     both = 2 * each
     pitch = columns.shape[0] // blocks
     gathered[...] = columns[...].astype(F32)
     edge = gathered[pl.ds(both, blocks, stride=pitch), :]
-    before = jnp.where(lax.broadcasted_iota(jnp.int32, edge.shape, 0) == 0, 0.0, pltpu.roll(edge, 1, 0))
+    deep = blocks // SIDE
+    wrapped = pltpu.roll(edge[blocks - deep :], 1, 0)
+    wrapped = jnp.where(lax.broadcasted_iota(jnp.int32, wrapped.shape, 0) == 0, 0.0, wrapped)
+    before = jnp.concatenate([wrapped, edge[: blocks - deep]], axis=0)
     featurized = edge + pltpu.roll(before, rows - 6, 1)
     edge_gate = featurized * pltpu.roll(featurized, rows - 2, 1)
     edge_query = pltpu.roll(featurized, rows - 4, 1)
-    edge_skip = pltpu.roll(edge, rows - 12, 1)
+    edge_skip = edge_query * edge_gate * pltpu.roll(edge, rows - 12, 1)
     lane = lax.broadcasted_iota(jnp.int32, edge.shape, 1)
 
     def channel(array, ch):
@@ -143,37 +155,31 @@
         re = outer[:blocks, ch * rows : (ch + 1) * rows]
         im = outer[blocks:, ch * rows : (ch + 1) * rows]
         twisted.append(jnp.concatenate([re * cos + im * sin, im * cos - re * sin], axis=1))
-    high, low = split(jnp.concatenate(twisted, axis=0))
-    spectrum = jnp.dot(jnp.concatenate([high, low, high], axis=1), forward[...], preferred_element_type=F32)
+    spectrum = transform(jnp.concatenate(twisted, axis=0), forward)
     gate, filt = spectrum[: each * blocks], spectrum[each * blocks :]
     gate_re, gate_im = gate[:, :rows], gate[:, rows:]
     filt_re, filt_im = filt[:, :rows], filt[:, rows:]
-    product = jnp.concatenate(
-        [gate_re * filt_re - gate_im * filt_im, gate_re * filt_im + gate_im * filt_re], axis=1
-    )
-    high, low = split(product)
-    inner = jnp.dot(jnp.concatenate([high, low, high], axis=1), backward[...], preferred_element_type=F32)
+    product = [gate_re * filt_re - gate_im * filt_im, -gate_re * filt_im - gate_im * filt_re]
+    inner = transform(jnp.concatenate(product, axis=1), forward)
     turned = []
     for ch in range(each):
         re = inner[ch * blocks : (ch + 1) * blocks, :rows]
         im = inner[ch * blocks : (ch + 1) * blocks, rows:]
-        turned.append(jnp.concatenate([re * cos - im * sin, re * sin + im * cos], axis=0))
+        turned.append(jnp.concatenate([re * cos + im * sin, re * sin - im * cos], axis=0))
     high, low = split(jnp.concatenate(turned, axis=1))
     result = jnp.dot(last[...], jnp.concatenate([high, low, high], axis=0), preferred_element_type=F32)
     for ch in range(each):
         part = result[:, ch * rows : (ch + 1) * rows]
-        scale = channel(edge_skip, ch)
-        scale = jnp.where(lane == 1, pltpu.roll(scale, 1, 1), scale)
-        finished = channel(edge_query, ch) * (part + scale * channel(edge_gate, ch))
+        finished = channel(edge_query, ch) * part + channel(edge_skip, ch)
         spread[pl.ds(ch, blocks, stride=each), :] = jnp.where(lane < 2, finished, part)
     out[...] = spread[...].reshape(out.shape).astype(out.dtype)
 
 
 def give_kernel(conv, query, skip, weight, gated, given):
-    arrived = conv[...].astype(F32).reshape(query.shape)
-    row = lax.broadcasted_iota(jnp.int32, query.shape, 1)
+    arrived = conv[...].astype(F32).reshape(query.shape[::-1]).T
+    row = lax.broadcasted_iota(jnp.int32, query.shape, 0)
     finished = jnp.where(row < 2, arrived, query[...] * (arrived + skip[...]))
-    gated[...] = finished.T.astype(gated.dtype)
+    gated[...] = finished.astype(gated.dtype)
     for y in range(given.shape[0]):
         given[y] = jnp.dot(gated[...], weight[y], preferred_element_type=F32).astype(given.dtype)
 
@@ -200,6 +206,7 @@
     shares = lax.axis_size("tp")
     chips = shares // 2
     each = width // blocks
+    order = [[int(block) for block in block_order(blocks)]]
     cols = out_weight.shape[1] // shares
     consts = [jnp.asarray(table) for table in tables(blocks, rows)]
     planes = jnp.transpose(features, (1, 0, 2))
@@ -209,8 +216,8 @@
         functools.partial(short_kernel, len(staged)),
         out_shape=(
             jax.ShapeDtypeStruct((blocks * pitch, rows), BF16),
-            jax.ShapeDtypeStruct((width, rows), F32),
-            jax.ShapeDtypeStruct((width, rows), F32),
+            jax.ShapeDtypeStruct((rows, width), F32),
+            jax.ShapeDtypeStruct((rows, width), F32),
             jax.ShapeDtypeStruct((chips, width, cols), BF16),
             *(jax.ShapeDtypeStruct(array.shape, array.dtype) for array in consts),
         ),
@@ -226,12 +233,12 @@
         name="short",
     )(*(pltpu.with_memory_space_constraint(array, pltpu.HBM) for array in staged))
     send = send.reshape(blocks, pitch // 2, 2, rows)
-    columns = lax.all_to_all(send, "ctx", split_axis=0, concat_axis=0, tiled=True)
+    columns = lax.all_to_all(send, "ctx", split_axis=0, concat_axis=0, tiled=True, axis_index_groups=order)
     columns = columns.reshape(blocks * pitch, rows)
     conv = pl.pallas_call(
         conv_kernel,
         out_shape=jax.ShapeDtypeStruct((blocks, each, rows), BF16),
-        in_specs=[VMEM] * 6,
+        in_specs=[VMEM] * 5,
         out_specs=VMEM,
         scratch_shapes=[
             pltpu.VMEM((blocks * pitch, rows), F32),
@@ -240,7 +247,7 @@
         compiler_params=PARAMS,
         name="conv",
     )(columns, *consts)
-    conv = lax.all_to_all(conv, "ctx", split_axis=0, concat_axis=0, tiled=True)
+    conv = lax.all_to_all(conv, "ctx", split_axis=0, concat_axis=0, tiled=True, axis_index_groups=order)
     gated, given = pl.pallas_call(
         give_kernel,
         out_shape=(

time: 88.2 us -> 86.8 us (0.984)
  blocking collectives: 75 us -> 74.1 us
    all_to_all x2, blocking collectives: 61.7 us -> 60.8 us  [the longest x1 38.9 us: body(): lax.all_to_all(send, 'ctx', split_axis=0, concat_axis=0, tiled=True, axis...]
where the time goes in v5:
time: 86.8 us; the launch traced here: 86.5 us
  blocking collectives  74.1 us (85%)
  Pallas kernels  7.23 us (8%)
  starting transfers between devices  5.17 us (6%)
    all_to_all x1, blocking collectives, body(): lax.all_to_all(send, 'ctx', split_axis=0, concat_axis=0, tiled=True, axis...  38.9 us
    all_to_all x1, blocking collectives, body(): lax.all_to_all(conv, 'ctx', split_axis=0, concat_axis=0, tiled=True, axis...  21.8 us
    all_to_all x1, blocking collectives, body(): lax.all_to_all(partial, 'tp', split_axis=0, concat_axis=0, tiled=True, ax...  13.3 us
    ppermute x1, starting transfers between devices, body(): arrived = lax.ppermute(given, 'tp', [(i, i ^ 1) for i in range(shares)])  5.17 us
    pallas_call x1, Pallas kernels, body(): pl.pallas_call(keep_kernel, out_shape=jax.ShapeDtypeStruct((chips, rows,...  2.03 us
    pallas_call x1, Pallas kernels, body(): pl.pallas_call(functools.partial(short_kernel, len(staged)), out_shape=(j...  1.99 us
    pallas_call x1, Pallas kernels, body(): pl.pallas_call(conv_kernel, out_shape=jax.ShapeDtypeStruct((blocks, each,...  1.91 us
  transfers between devices with their start and end apart: 1, of which 0 were waited for; matrix products, arithmetic and copies ran while one was open for 0% of the time, Pallas kernels for 2%

profile of v5, /device:TPU:1, one launch (start us, length us, event | category | flops | bytes accessed | tf_op | source)
XLA Modules:
  0.0 86.5 jit_solution(4404517747394409803)
XLA Ops:
  0.0 2.0 %short.1 = (bf16[1152,128]{1,0:T(8,128)(2,1)S(1)}, f32[128,512]{1,0:T(8,128)S(1)}, f32[128,512]{1,0:T(8,128)S(1)}, bf16[4,512,512]{2,1,0:T(8,128)(2,1)S(1)}, bf1...) custom-call(bf16[3,128,512]{2,1,0:T(8,128)(2,1)} %bitcast.6, ...), custom_call_target="tpu_custom_call" | custom-call | tf_op jit(solution)/shard_map/short/pallas_call | solution.py:215
  2.0 38.9 %all_to_all.15 = bf16[64,9,2,128]{3,2,1,0:T(2,128)(2,1)S(1)} all-to-all(bf16[64,9,2,128]{3,2,1,0:T(2,128)(2,1)S(1)} %bitcast.5), channel_id=1, replica_groups={{0,32,64,96,128,160,192,224,256,288,320,352,384,416,448,480,8,40,72,104..., dimensions={0} | all-to-all | bytes 589824 | tf_op jit(solution)/shard_map/all_to_all | solution.py:236
  40.9 1.9 %conv.1 = bf16[64,8,128]{2,1,0:T(8,128)(2,1)S(1)} custom-call(bf16[1152,128]{1,0:T(8,128)(2,1)S(1)} %bitcast.4, bf16[128,128]{1,0:T(8,128)(2,1)S(1)} %get-tuple-element.16.first, f32[2,64,128]{2,1,0:T(8,128)S(1)} %get-tuple-element.17.twist, bf16[2,256,256]{2,1,0:T(8,128)(2,1)S(1)} %get-tuple-element.18.forward, bf16[64,384]{1,0:T(8,128)(2,1)S(1)} %get-tuple-element.19.last), custom_call_target="tpu_custom_call" | custom-call | tf_op jit(solution)/shard_map/conv/pallas_call | solution.py:238
  42.9 21.8 %all_to_all.16.conv = bf16[64,8,128]{2,1,0:T(8,128)(2,1)S(1)} all-to-all(bf16[64,8,128]{2,1,0:T(8,128)(2,1)S(1)} %conv.1), channel_id=1, replica_groups={{0,32,64,96,128,160,192,224,256,288,320,352,384,416,448,480,8,40,72,104..., dimensions={0} | all-to-all | bytes 262144 | tf_op jit(solution)/shard_map/all_to_all | solution.py:250
  64.7 0.5 give.1
  65.2 5.2 %collective-permute-start = (bf16[4,128,512]{2,1,0:T(8,128)(2,1)S(1)}, bf16[4,128,512]{2,1,0:T(8,128)(2,1)S(1)}, u32[]{:S(2)}, u32[]{:S(2)}) collective-permute-start(bf16[4,128,512]{2,1,0:T(8,128)(2,1)S(1)} %get-tuple-element.24), channel_id=1, source_target_pairs={{0,1},{1,0},{2,3},{3,2},{4,5},{5,4},{6,7},{7,6},{8,9},{9,8},{10,11... | collective-permute-start | bytes 1572872 | tf_op jit(solution)/shard_map/ppermute | solution.py:262
  70.3 2.0 %keep.1.kept = f32[4,128,512]{2,1,0:T(8,128)S(1)} custom-call(bf16[128,512]{1,0:T(8,128)(2,1)S(1)} %get-tuple-element.23.gated, bf16[512,4096]{1,0:T(8,128)(2,1)} %weight.1), custom_call_target="tpu_custom_call" | custom-call | tf_op jit(solution)/shard_map/keep/pallas_call | solution.py:263
  72.4 0.0 collective-permute-done.arrived
  72.4 0.1 pair.1
  72.5 13.3 %all_to_all.17.parts = bf16[4,128,512]{2,1,0:T(8,128)(2,1)S(1)} all-to-all(bf16[4,128,512]{2,1,0:T(8,128)(2,1)S(1)} %pair.1), channel_id=1, replica_groups={{0,2,4,6},{1,3,5,7},{8,10,12,14},{9,11,13,15},{16,18,20,22},{17,19,21,2..., dimensions={0} | all-to-all | bytes 1048576 | tf_op jit(solution)/shard_map/all_to_all | solution.py:281
  85.8 0.7 total.1
Async XLA Ops:
  65.2 7.2 %collective-permute-start = (bf16[4,128,512]{2,1,0:T(8,128)(2,1)S(1)}, bf16[4,128,512]{2,1,0:T(8,128)(2,1)S(1)}, u32[]{:S(2)}, u32[]{:S(2)}) collective-permute-start(bf16[4,128,512]{2,1,0:T(8,128)(2,1)S(1)} %get-tuple-element.24), channel_id=1, source_target_pairs={{0,1},{1,0},{2,3},{3,2},{4,5},{5,4},{6,7},{7,6},{8,9},{9,8},{10,11... | collective-permute-start | bytes 1572872 | tf_op jit(solution)/shard_map/ppermute | solution.py:262

commit v6 on v5

--- a/solution.py
+++ b/solution.py
@@ -24,7 +24,9 @@
 
 
 def block_order(blocks):
-    return np.arange(blocks).reshape(-1, SIDE).T.reshape(-1)
+    deep = blocks // SIDE
+    z = (np.arange(deep)[::-1] + 5 * deep // 8) % deep
+    return (SIDE * z[None, :] + np.arange(SIDE)[::-1][:, None]).reshape(-1)
 
 
 def tables(blocks, rows):
@@ -38,10 +40,13 @@
     inner = 2.0 * math.pi * (np.outer(np.arange(rows), np.arange(rows)) % rows) / rows
     cos, sin = np.cos(inner), np.sin(inner)
     forward = np.block([[cos, -sin], [sin, cos]]).astype(np.float32)
+    order = block_order(blocks)
+    previous = (order[:, None] == order[None, :] + 1).astype(BF16)
     first_hi, first_lo = halves(first)
     last_hi, last_lo = halves(last)
     forward_hi, forward_lo = halves(forward)
     return (
+        previous,
         np.concatenate([first_hi, first_lo], axis=1),
         twist,
         np.stack([forward_hi, forward_lo]),
@@ -74,7 +79,7 @@
 def columns_of_core(weight, chips, partner):
     cols = weight.shape[1] // (2 * chips)
     core = lax.rem(lax.axis_index("tp") + partner, 2)
-    return [weight.at[:, pl.ds(pl.multiple_of((2 * y + core) * cols, cols), cols)] for y in range(chips)]
+    return [weight.at[:, pl.ds(pl.multiple_of((2 * y + core) * cols, cols), cols)] for y in reversed(range(chips))]
 
 
 def short_kernel(count, *refs):
@@ -125,16 +130,13 @@
         copy.wait()
 
 
-def conv_kernel(columns, first, twist, forward, last, out, gathered, spread):
+def conv_kernel(columns, previous, first, twist, forward, last, out, gathered, spread):
     each, blocks, rows = RIM // 2, out.shape[0], out.shape[2]
     both = 2 * each
     pitch = columns.shape[0] // blocks
     gathered[...] = columns[...].astype(F32)
     edge = gathered[pl.ds(both, blocks, stride=pitch), :]
-    deep = blocks // SIDE
-    wrapped = pltpu.roll(edge[blocks - deep :], 1, 0)
-    wrapped = jnp.where(lax.broadcasted_iota(jnp.int32, wrapped.shape, 0) == 0, 0.0, wrapped)
-    before = jnp.concatenate([wrapped, edge[: blocks - deep]], axis=0)
+    before = jnp.dot(previous[...], edge.astype(BF16), preferred_element_type=F32)
     featurized = edge + pltpu.roll(before, rows - 6, 1)
     edge_gate = featurized * pltpu.roll(featurized, rows - 2, 1)
     edge_query = pltpu.roll(featurized, rows - 4, 1)
@@ -238,7 +240,7 @@
     conv = pl.pallas_call(
         conv_kernel,
         out_shape=jax.ShapeDtypeStruct((blocks, each, rows), BF16),
-        in_specs=[VMEM] * 5,
+        in_specs=[VMEM] * 6,
         out_specs=VMEM,
         scratch_shapes=[
             pltpu.VMEM((blocks * pitch, rows), F32),
@@ -277,7 +279,7 @@
         compiler_params=PARAMS,
         name="pair",
     )(kept, arrived)
-    columns_of = [[2 * y + core for y in range(chips)] for core in range(2)]
+    columns_of = [[2 * y + core for y in reversed(range(chips))] for core in range(2)]
     partial = lax.all_to_all(
         partial, "tp", split_axis=0, concat_axis=0, tiled=True, axis_index_groups=columns_of
     )

time: 86.8 us -> 80.4 us (0.926)
  blocking collectives: 74.1 us -> 68 us
    all_to_all x1, blocking collectives: 38.9 us -> 35.3 us  [body(): lax.all_to_all(send, 'ctx', split_axis=0, concat_axis=0, tiled=True, axis...]
    all_to_all x1, blocking collectives: 21.8 us -> 20 us  [body(): lax.all_to_all(conv, 'ctx', split_axis=0, concat_axis=0, tiled=True, axis...]
  transfers between devices with their start and end apart: 1 -> 1, of which waited for: 0 -> 0; matrix products, arithmetic and copies ran while one was open for 0% -> 0% of each run, Pallas kernels for 2% -> 3%
where the time goes in v6:
time: 80.4 us; the launch traced here: 80.2 us
  blocking collectives  68 us (85%)
  Pallas kernels  7.45 us (9%)
  starting transfers between devices  4.64 us (6%)
    all_to_all x1, blocking collectives, body(): lax.all_to_all(send, 'ctx', split_axis=0, concat_axis=0, tiled=True, axis...  35.3 us
    all_to_all x1, blocking collectives, body(): lax.all_to_all(conv, 'ctx', split_axis=0, concat_axis=0, tiled=True, axis...  20 us
    all_to_all x1, blocking collectives, body(): lax.all_to_all(partial, 'tp', split_axis=0, concat_axis=0, tiled=True, ax...  12.7 us
    ppermute x1, starting transfers between devices, body(): arrived = lax.ppermute(given, 'tp', [(i, i ^ 1) for i in range(shares)])  4.64 us
    pallas_call x1, Pallas kernels, body(): pl.pallas_call(conv_kernel, out_shape=jax.ShapeDtypeStruct((blocks, each,...  2.11 us
    pallas_call x1, Pallas kernels, body(): pl.pallas_call(keep_kernel, out_shape=jax.ShapeDtypeStruct((chips, rows,...  2.03 us
    pallas_call x1, Pallas kernels, body(): pl.pallas_call(functools.partial(short_kernel, len(staged)), out_shape=(j...  2.02 us
  transfers between devices with their start and end apart: 1, of which 0 were waited for; matrix products, arithmetic and copies ran while one was open for 0% of the time, Pallas kernels for 3%

profile of v6, /device:TPU:1, one launch (start us, length us, event | category | flops | bytes accessed | tf_op | source)
XLA Modules:
  0.0 80.2 jit_solution(10219596858615950161)
XLA Ops:
  0.0 2.0 %short.1 = (bf16[1152,128]{1,0:T(8,128)(2,1)S(1)}, f32[128,512]{1,0:T(8,128)S(1)}, f32[128,512]{1,0:T(8,128)S(1)}, bf16[4,512,512]{2,1,0:T(8,128)(2,1)S(1)}, bf1...) custom-call(bf16[3,128,512]{2,1,0:T(8,128)(2,1)} %bitcast.6, ...), custom_call_target="tpu_custom_call" | custom-call | tf_op jit(solution)/shard_map/short/pallas_call | solution.py:217
  2.0 35.3 %all_to_all.15 = bf16[64,9,2,128]{3,2,1,0:T(2,128)(2,1)S(1)} all-to-all(bf16[64,9,2,128]{3,2,1,0:T(2,128)(2,1)S(1)} %bitcast.5), channel_id=1, replica_groups={{312,280,248,216,184,152,120,88,56,24,504,472,440,408,376,344,304,272,2..., dimensions={0} | all-to-all | bytes 589824 | tf_op jit(solution)/shard_map/all_to_all | solution.py:238
  37.3 2.1 %conv.1 = bf16[64,8,128]{2,1,0:T(8,128)(2,1)S(1)} custom-call(bf16[1152,128]{1,0:T(8,128)(2,1)S(1)} %bitcast.4, bf16[64,64]{1,0:T(8,128)(2,1)S(1)} %get-tuple-element.17.previous, bf16[128,128]{1,0:T(8,128)(2,1)S(1)} %get-tuple-element.18.first, f32[2,64,128]{2,1,0:T(8,128)S(1)} %get-tuple-element.19.twist, ...), custom_call_target="tpu_custom_call" | custom-call | tf_op jit(solution)/shard_map/conv/pallas_call | solution.py:240
  39.5 20.0 %all_to_all.16.conv = bf16[64,8,128]{2,1,0:T(8,128)(2,1)S(1)} all-to-all(bf16[64,8,128]{2,1,0:T(8,128)(2,1)S(1)} %conv.1), channel_id=1, replica_groups={{312,280,248,216,184,152,120,88,56,24,504,472,440,408,376,344,304,272,2..., dimensions={0} | all-to-all | bytes 262144 | tf_op jit(solution)/shard_map/all_to_all | solution.py:252
  59.5 0.5 give.1
  60.0 4.6 %collective-permute-start = (bf16[4,128,512]{2,1,0:T(8,128)(2,1)S(1)}, bf16[4,128,512]{2,1,0:T(8,128)(2,1)S(1)}, u32[]{:S(2)}, u32[]{:S(2)}) collective-permute-start(bf16[4,128,512]{2,1,0:T(8,128)(2,1)S(1)} %get-tuple-element.26), channel_id=1, source_target_pairs={{0,1},{1,0},{2,3},{3,2},{4,5},{5,4},{6,7},{7,6},{8,9},{9,8},{10,11... | collective-permute-start | bytes 1572872 | tf_op jit(solution)/shard_map/ppermute | solution.py:264
  64.6 2.0 %keep.1.kept = f32[4,128,512]{2,1,0:T(8,128)S(1)} custom-call(bf16[128,512]{1,0:T(8,128)(2,1)S(1)} %get-tuple-element.25.gated, bf16[512,4096]{1,0:T(8,128)(2,1)} %weight.1), custom_call_target="tpu_custom_call" | custom-call | tf_op jit(solution)/shard_map/keep/pallas_call | solution.py:265
  66.7 0.0 collective-permute-done.arrived
  66.7 0.1 pair.1
  66.8 12.7 %all_to_all.17.parts = bf16[4,128,512]{2,1,0:T(8,128)(2,1)S(1)} all-to-all(bf16[4,128,512]{2,1,0:T(8,128)(2,1)S(1)} %pair.1), channel_id=1, replica_groups={{6,4,2,0},{7,5,3,1},{14,12,10,8},{15,13,11,9},{22,20,18,16},{23,21,19,1..., dimensions={0} | all-to-all | bytes 1048576 | tf_op jit(solution)/shard_map/all_to_all | solution.py:283
  79.5 0.7 total.1
Async XLA Ops:
  60.0 6.7 %collective-permute-start = (bf16[4,128,512]{2,1,0:T(8,128)(2,1)S(1)}, bf16[4,128,512]{2,1,0:T(8,128)(2,1)S(1)}, u32[]{:S(2)}, u32[]{:S(2)}) collective-permute-start(bf16[4,128,512]{2,1,0:T(8,128)(2,1)S(1)} %get-tuple-element.26), channel_id=1, source_target_pairs={{0,1},{1,0},{2,3},{3,2},{4,5},{5,4},{6,7},{7,6},{8,9},{9,8},{10,11... | collective-permute-start | bytes 1572872 | tf_op jit(solution)/shard_map/ppermute | solution.py:264

commit v7 on v5

--- a/solution.py
+++ b/solution.py
@@ -14,6 +14,7 @@
 VMEM = pl.BlockSpec(memory_space=pltpu.VMEM)
 RIM = 16
 SIDE = 4
+X_ORDER = (3, 2, 1, 0)
 PARAMS = pltpu.CompilerParams(vmem_limit_bytes=24 * 1024 * 1024)
 
 
@@ -23,8 +24,13 @@
     return high, low
 
 
+def z_order(deep):
+    return (np.arange(deep)[::-1] + 5 * deep // 8) % deep
+
+
 def block_order(blocks):
-    return np.arange(blocks).reshape(-1, SIDE).T.reshape(-1)
+    z = z_order(blocks // SIDE)
+    return (SIDE * z[None, :] + np.array(X_ORDER)[:, None]).reshape(-1)
 
 
 def tables(blocks, rows):
@@ -74,7 +80,7 @@
 def columns_of_core(weight, chips, partner):
     cols = weight.shape[1] // (2 * chips)
     core = lax.rem(lax.axis_index("tp") + partner, 2)
-    return [weight.at[:, pl.ds(pl.multiple_of((2 * y + core) * cols, cols), cols)] for y in range(chips)]
+    return [weight.at[:, pl.ds(pl.multiple_of((2 * y + core) * cols, cols), cols)] for y in reversed(range(chips))]
 
 
 def short_kernel(count, *refs):
@@ -132,9 +138,10 @@
     gathered[...] = columns[...].astype(F32)
     edge = gathered[pl.ds(both, blocks, stride=pitch), :]
     deep = blocks // SIDE
-    wrapped = pltpu.roll(edge[blocks - deep :], 1, 0)
-    wrapped = jnp.where(lax.broadcasted_iota(jnp.int32, wrapped.shape, 0) == 0, 0.0, wrapped)
-    before = jnp.concatenate([wrapped, edge[: blocks - deep]], axis=0)
+    runs = {x: edge[deep * i : deep * (i + 1)] for i, x in enumerate(X_ORDER)}
+    start = lax.broadcasted_iota(jnp.int32, (deep, rows), 0) == z_order(deep).tolist().index(0)
+    wrapped = jnp.where(start, 0.0, pltpu.roll(runs[SIDE - 1], deep - 1, 0))
+    before = jnp.concatenate([runs[x - 1] if x else wrapped for x in X_ORDER], axis=0)
     featurized = edge + pltpu.roll(before, rows - 6, 1)
     edge_gate = featurized * pltpu.roll(featurized, rows - 2, 1)
     edge_query = pltpu.roll(featurized, rows - 4, 1)
@@ -277,7 +284,7 @@
         compiler_params=PARAMS,
         name="pair",
     )(kept, arrived)
-    columns_of = [[2 * y + core for y in range(chips)] for core in range(2)]
+    columns_of = [[2 * y + core for y in reversed(range(chips))] for core in range(2)]
     partial = lax.all_to_all(
         partial, "tp", split_axis=0, concat_axis=0, tiled=True, axis_index_groups=columns_of
     )

time: 86.8 us -> 80.2 us (0.924)
  blocking collectives: 74.1 us -> 68 us
    all_to_all x1, blocking collectives: 38.9 us -> 35.3 us  [body(): lax.all_to_all(send, 'ctx', split_axis=0, concat_axis=0, tiled=True, axis...]
    all_to_all x1, blocking collectives: 21.8 us -> 20 us  [body(): lax.all_to_all(conv, 'ctx', split_axis=0, concat_axis=0, tiled=True, axis...]
  transfers between devices with their start and end apart: 1 -> 1, of which waited for: 0 -> 0; matrix products, arithmetic and copies ran while one was open for 0% -> 0% of each run, Pallas kernels for 2% -> 3%
where the time goes in v7:
time: 80.2 us; the launch traced here: 80 us
  blocking collectives  68 us (85%)
  Pallas kernels  7.24 us (9%)
  starting transfers between devices  4.64 us (6%)
    all_to_all x1, blocking collectives, body(): lax.all_to_all(send, 'ctx', split_axis=0, concat_axis=0, tiled=True, axis...  35.3 us
    all_to_all x1, blocking collectives, body(): lax.all_to_all(conv, 'ctx', split_axis=0, concat_axis=0, tiled=True, axis...  20 us
    all_to_all x1, blocking collectives, body(): lax.all_to_all(partial, 'tp', split_axis=0, concat_axis=0, tiled=True, ax...  12.7 us
    ppermute x1, starting transfers between devices, body(): arrived = lax.ppermute(given, 'tp', [(i, i ^ 1) for i in range(shares)])  4.64 us
    pallas_call x1, Pallas kernels, body(): pl.pallas_call(keep_kernel, out_shape=jax.ShapeDtypeStruct((chips, rows,...  2.03 us
    pallas_call x1, Pallas kernels, body(): pl.pallas_call(functools.partial(short_kernel, len(staged)), out_shape=(j...  1.99 us
    pallas_call x1, Pallas kernels, body(): pl.pallas_call(conv_kernel, out_shape=jax.ShapeDtypeStruct((blocks, each,...  1.92 us
  transfers between devices with their start and end apart: 1, of which 0 were waited for; matrix products, arithmetic and copies ran while one was open for 0% of the time, Pallas kernels for 3%

profile of v7, /device:TPU:1, one launch (start us, length us, event | category | flops | bytes accessed | tf_op | source)
XLA Modules:
  0.0 80.0 jit_solution(18191073355240428761)
XLA Ops:
  0.0 2.0 %short.1 = (bf16[1152,128]{1,0:T(8,128)(2,1)S(1)}, f32[128,512]{1,0:T(8,128)S(1)}, f32[128,512]{1,0:T(8,128)S(1)}, bf16[4,512,512]{2,1,0:T(8,128)(2,1)S(1)}, bf1...) custom-call(bf16[3,128,512]{2,1,0:T(8,128)(2,1)} %bitcast.6, ...), custom_call_target="tpu_custom_call" | custom-call | tf_op jit(solution)/shard_map/short/pallas_call | solution.py:222
  2.0 35.3 %all_to_all.15 = bf16[64,9,2,128]{3,2,1,0:T(2,128)(2,1)S(1)} all-to-all(bf16[64,9,2,128]{3,2,1,0:T(2,128)(2,1)S(1)} %bitcast.5), channel_id=1, replica_groups={{312,280,248,216,184,152,120,88,56,24,504,472,440,408,376,344,304,272,2..., dimensions={0} | all-to-all | bytes 589824 | tf_op jit(solution)/shard_map/all_to_all | solution.py:243
  37.3 1.9 %conv.1 = bf16[64,8,128]{2,1,0:T(8,128)(2,1)S(1)} custom-call(bf16[1152,128]{1,0:T(8,128)(2,1)S(1)} %bitcast.4, bf16[128,128]{1,0:T(8,128)(2,1)S(1)} %get-tuple-element.16.first, f32[2,64,128]{2,1,0:T(8,128)S(1)} %get-tuple-element.17.twist, bf16[2,256,256]{2,1,0:T(8,128)(2,1)S(1)} %get-tuple-element.18.forward, bf16[64,384]{1,0:T(8,128)(2,1)S(1)} %get-tuple-element.19.last), custom_call_target="tpu_custom_call" | custom-call | tf_op jit(solution)/shard_map/conv/pallas_call | solution.py:245
  39.2 20.0 %all_to_all.16.conv = bf16[64,8,128]{2,1,0:T(8,128)(2,1)S(1)} all-to-all(bf16[64,8,128]{2,1,0:T(8,128)(2,1)S(1)} %conv.1), channel_id=1, replica_groups={{312,280,248,216,184,152,120,88,56,24,504,472,440,408,376,344,304,272,2..., dimensions={0} | all-to-all | bytes 262144 | tf_op jit(solution)/shard_map/all_to_all | solution.py:257
  59.3 0.5 give.1
  59.8 4.6 %collective-permute-start = (bf16[4,128,512]{2,1,0:T(8,128)(2,1)S(1)}, bf16[4,128,512]{2,1,0:T(8,128)(2,1)S(1)}, u32[]{:S(2)}, u32[]{:S(2)}) collective-permute-start(bf16[4,128,512]{2,1,0:T(8,128)(2,1)S(1)} %get-tuple-element.24), channel_id=1, source_target_pairs={{0,1},{1,0},{2,3},{3,2},{4,5},{5,4},{6,7},{7,6},{8,9},{9,8},{10,11... | collective-permute-start | bytes 1572872 | tf_op jit(solution)/shard_map/ppermute | solution.py:269
  64.4 2.0 %keep.1.kept = f32[4,128,512]{2,1,0:T(8,128)S(1)} custom-call(bf16[128,512]{1,0:T(8,128)(2,1)S(1)} %get-tuple-element.23.gated, bf16[512,4096]{1,0:T(8,128)(2,1)} %weight.1), custom_call_target="tpu_custom_call" | custom-call | tf_op jit(solution)/shard_map/keep/pallas_call | solution.py:270
  66.4 0.0 collective-permute-done.arrived
  66.5 0.1 pair.1
  66.6 12.7 %all_to_all.17.parts = bf16[4,128,512]{2,1,0:T(8,128)(2,1)S(1)} all-to-all(bf16[4,128,512]{2,1,0:T(8,128)(2,1)S(1)} %pair.1), channel_id=1, replica_groups={{6,4,2,0},{7,5,3,1},{14,12,10,8},{15,13,11,9},{22,20,18,16},{23,21,19,1..., dimensions={0} | all-to-all | bytes 1048576 | tf_op jit(solution)/shard_map/all_to_all | solution.py:288
  79.2 0.7 total.1
Async XLA Ops:
  59.8 6.7 %collective-permute-start = (bf16[4,128,512]{2,1,0:T(8,128)(2,1)S(1)}, bf16[4,128,512]{2,1,0:T(8,128)(2,1)S(1)}, u32[]{:S(2)}, u32[]{:S(2)}) collective-permute-start(bf16[4,128,512]{2,1,0:T(8,128)(2,1)S(1)} %get-tuple-element.24), channel_id=1, source_target_pairs={{0,1},{1,0},{2,3},{3,2},{4,5},{5,4},{6,7},{7,6},{8,9},{9,8},{10,11... | collective-permute-start | bytes 1572872 | tf_op jit(solution)/shard_map/ppermute | solution.py:269

commit v8 on v7

--- a/solution.py
+++ b/solution.py
@@ -14,7 +14,7 @@
 VMEM = pl.BlockSpec(memory_space=pltpu.VMEM)
 RIM = 16
 SIDE = 4
-X_ORDER = (3, 2, 1, 0)
+X_ORDER = (2, 1, 0, 3)
 PARAMS = pltpu.CompilerParams(vmem_limit_bytes=24 * 1024 * 1024)
 
 

time: 80.2 us -> 79.7 us (level)
  no operation moved by 1% of the time
where the time goes in v8:
time: 79.7 us; the launch traced here: 79.4 us
  blocking collectives  67.7 us (85%)
  Pallas kernels  7.23 us (9%)
  starting transfers between devices  4.41 us (6%)
    all_to_all x1, blocking collectives, body(): lax.all_to_all(send, 'ctx', split_axis=0, concat_axis=0, tiled=True, axis...  35.3 us
    all_to_all x1, blocking collectives, body(): lax.all_to_all(conv, 'ctx', split_axis=0, concat_axis=0, tiled=True, axis...  19.7 us
    all_to_all x1, blocking collectives, body(): lax.all_to_all(partial, 'tp', split_axis=0, concat_axis=0, tiled=True, ax...  12.7 us
    ppermute x1, starting transfers between devices, body(): arrived = lax.ppermute(given, 'tp', [(i, i ^ 1) for i in range(shares)])  4.41 us
    pallas_call x1, Pallas kernels, body(): pl.pallas_call(keep_kernel, out_shape=jax.ShapeDtypeStruct((chips, rows,...  2.03 us
    pallas_call x1, Pallas kernels, body(): pl.pallas_call(functools.partial(short_kernel, len(staged)), out_shape=(j...  1.99 us
    pallas_call x1, Pallas kernels, body(): pl.pallas_call(conv_kernel, out_shape=jax.ShapeDtypeStruct((blocks, each,...  1.91 us
  transfers between devices with their start and end apart: 1, of which 0 were waited for; matrix products, arithmetic and copies ran while one was open for 0% of the time, Pallas kernels for 3%

profile of v8, /device:TPU:1, one launch (start us, length us, event | category | flops | bytes accessed | tf_op | source)
XLA Modules:
  0.0 79.4 jit_solution(17152264526142342531)
XLA Ops:
  0.0 2.0 %short.1 = (bf16[1152,128]{1,0:T(8,128)(2,1)S(1)}, f32[128,512]{1,0:T(8,128)S(1)}, f32[128,512]{1,0:T(8,128)S(1)}, bf16[4,512,512]{2,1,0:T(8,128)(2,1)S(1)}, bf1...) custom-call(bf16[3,128,512]{2,1,0:T(8,128)(2,1)} %bitcast.6, ...), custom_call_target="tpu_custom_call" | custom-call | tf_op jit(solution)/shard_map/short/pallas_call | solution.py:222
  2.0 35.3 %all_to_all.15 = bf16[64,9,2,128]{3,2,1,0:T(2,128)(2,1)S(1)} all-to-all(bf16[64,9,2,128]{3,2,1,0:T(2,128)(2,1)S(1)} %bitcast.5), channel_id=1, replica_groups={{304,272,240,208,176,144,112,80,48,16,496,464,432,400,368,336,296,264,2..., dimensions={0} | all-to-all | bytes 589824 | tf_op jit(solution)/shard_map/all_to_all | solution.py:243
  37.3 1.9 %conv.1 = bf16[64,8,128]{2,1,0:T(8,128)(2,1)S(1)} custom-call(bf16[1152,128]{1,0:T(8,128)(2,1)S(1)} %bitcast.4, bf16[128,128]{1,0:T(8,128)(2,1)S(1)} %get-tuple-element.16.first, f32[2,64,128]{2,1,0:T(8,128)S(1)} %get-tuple-element.17.twist, bf16[2,256,256]{2,1,0:T(8,128)(2,1)S(1)} %get-tuple-element.18.forward, bf16[64,384]{1,0:T(8,128)(2,1)S(1)} %get-tuple-element.19.last), custom_call_target="tpu_custom_call" | custom-call | tf_op jit(solution)/shard_map/conv/pallas_call | solution.py:245
  39.2 19.7 %all_to_all.16.conv = bf16[64,8,128]{2,1,0:T(8,128)(2,1)S(1)} all-to-all(bf16[64,8,128]{2,1,0:T(8,128)(2,1)S(1)} %conv.1), channel_id=1, replica_groups={{304,272,240,208,176,144,112,80,48,16,496,464,432,400,368,336,296,264,2..., dimensions={0} | all-to-all | bytes 262144 | tf_op jit(solution)/shard_map/all_to_all | solution.py:257
  58.9 0.5 give.1
  59.4 4.4 %collective-permute-start = (bf16[4,128,512]{2,1,0:T(8,128)(2,1)S(1)}, bf16[4,128,512]{2,1,0:T(8,128)(2,1)S(1)}, u32[]{:S(2)}, u32[]{:S(2)}) collective-permute-start(bf16[4,128,512]{2,1,0:T(8,128)(2,1)S(1)} %get-tuple-element.24), channel_id=1, source_target_pairs={{0,1},{1,0},{2,3},{3,2},{4,5},{5,4},{6,7},{7,6},{8,9},{9,8},{10,11... | collective-permute-start | bytes 1572872 | tf_op jit(solution)/shard_map/ppermute | solution.py:269
  63.8 2.0 %keep.1.kept = f32[4,128,512]{2,1,0:T(8,128)S(1)} custom-call(bf16[128,512]{1,0:T(8,128)(2,1)S(1)} %get-tuple-element.23.gated, bf16[512,4096]{1,0:T(8,128)(2,1)} %weight.1), custom_call_target="tpu_custom_call" | custom-call | tf_op jit(solution)/shard_map/keep/pallas_call | solution.py:270
  65.9 0.0 collective-permute-done.arrived
  65.9 0.1 pair.1
  66.0 12.7 %all_to_all.17.parts = bf16[4,128,512]{2,1,0:T(8,128)(2,1)S(1)} all-to-all(bf16[4,128,512]{2,1,0:T(8,128)(2,1)S(1)} %pair.1), channel_id=1, replica_groups={{6,4,2,0},{7,5,3,1},{14,12,10,8},{15,13,11,9},{22,20,18,16},{23,21,19,1..., dimensions={0} | all-to-all | bytes 1048576 | tf_op jit(solution)/shard_map/all_to_all | solution.py:288
  78.7 0.7 total.1
Async XLA Ops:
  59.4 6.5 %collective-permute-start = (bf16[4,128,512]{2,1,0:T(8,128)(2,1)S(1)}, bf16[4,128,512]{2,1,0:T(8,128)(2,1)S(1)}, u32[]{:S(2)}, u32[]{:S(2)}) collective-permute-start(bf16[4,128,512]{2,1,0:T(8,128)(2,1)S(1)} %get-tuple-element.24), channel_id=1, source_target_pairs={{0,1},{1,0},{2,3},{3,2},{4,5},{5,4},{6,7},{7,6},{8,9},{9,8},{10,11... | collective-permute-start | bytes 1572872 | tf_op jit(solution)/shard_map/ppermute | solution.py:269
